TPU v7x, 512 devices: a whole 4x4x16 slice. The times are simulated.
512 devices in a mesh: wide: 32 (over x, z_hi, core), narrow: 16 (over z_lo, y).
Axes of the slice: x: 4, y: 4, z: 16 (z_hi: 4, z_lo: 4; z = z_hi * 4 + z_lo), core: 2. Of those that a mesh axis runs over, the one named last changes fastest.
Arguments:
- source: float32 [512, 512, 128], P(('wide', 'narrow')), may hold values from -6 to 6
- pressure_start: float32 [512, 512, 128], P(('wide', 'narrow')), may hold values from -6 to 6
- trans_x: float32 [512, 512, 128], P(('wide', 'narrow')), may hold values from 0.1 to 10
- trans_y: float32 [512, 512, 128], P(('wide', 'narrow')), may hold values from 0.1 to 10
- trans_z: float32 [512, 512, 128], P(('wide', 'narrow')), may hold values from 0.1 to 4
- storage: float32 [512, 512, 128], P(('wide', 'narrow')), may hold values from 0.2 to 2
- adjoint_seed: float32 [512, 512, 128], P(('wide', 'narrow')), may hold values from -6 to 6
- comp_cell: int32 [512, 64], P(('wide', 'narrow')), may hold values from 0 to 65535
- comp_well: int32 [512, 64], P(('wide', 'narrow')), may hold values from 0 to 20479
- comp_count: int32 [512], P(('wide', 'narrow')), may hold values from 1 to 64, as said below
- well_slot: int32 [20480], replicated, may hold values from 0 to 20479, each once
Outputs:
- grad_source: float32 [512, 512, 128], P(('wide', 'narrow'))
- well_sens: float32 [20480], P(('wide', 'narrow'))
Inputs may be any that keep to these rules, and one draw needn't show every extreme that they name: `comp_count`: every row has at least one live slot, and some row has all 64 live.
All inputs are finite; a program needn't handle non-finite values.
Results may differ from a plain program's by a relative error of at most 0.0003.
Values sent between devices are 32-bit elements; how exact they have to be, the bound alone decides.
A program may use at most 128 MiB of HBM per device.

v0:
```python
import jax
import jax.numpy as jnp
from jax import lax
from jax.sharding import PartitionSpec as P

ITERS = 2


def shifted(values, offset, axis_dim):
    extent = values.shape[axis_dim]
    if offset > 0:
        kept = lax.slice_in_dim(values, 0, extent - offset, axis=axis_dim)
        zero_part = jnp.zeros_like(lax.slice_in_dim(values, 0, offset, axis=axis_dim))
        return jnp.concatenate([zero_part, kept], axis=axis_dim)
    kept = lax.slice_in_dim(values, -offset, extent, axis=axis_dim)
    zero_part = jnp.zeros_like(lax.slice_in_dim(values, 0, -offset, axis=axis_dim))
    return jnp.concatenate([kept, zero_part], axis=axis_dim)


def factor_lines(trans, storage, axis_dim):
    extent = trans.shape[axis_dim]
    lower_band = -shifted(trans, 1, axis_dim)
    upper_band = -trans
    middle = storage + trans + shifted(trans, 1, axis_dim)
    factors = []
    stride = 1
    while stride < extent:
        below_mid = shifted(middle - 1.0, stride, axis_dim) + 1.0
        above_mid = shifted(middle - 1.0, -stride, axis_dim) + 1.0
        left_gain = lower_band / below_mid
        right_gain = upper_band / above_mid
        new_lower = -left_gain * shifted(lower_band, stride, axis_dim)
        new_upper = -right_gain * shifted(upper_band, -stride, axis_dim)
        middle = (
            middle
            - left_gain * shifted(upper_band, stride, axis_dim)
            - right_gain * shifted(lower_band, -stride, axis_dim)
        )
        lower_band, upper_band = (new_lower, new_upper)
        factors.append((stride, left_gain, right_gain))
        stride = stride * 2
    return (factors, middle)


def solve_lines(factored, right_side, axis_dim):
    factors, middle = factored
    for stride, left_gain, right_gain in factors:
        right_side = (
            right_side
            - left_gain * shifted(right_side, stride, axis_dim)
            - right_gain * shifted(right_side, -stride, axis_dim)
        )
    return right_side / middle


def divergence(values, trans, axis_dim):
    face_flux = trans * (values - shifted(values, -1, axis_dim))
    return face_flux - shifted(face_flux, 1, axis_dim)


def face_product(first_field, second_field, axis_dim):
    return (first_field - shifted(first_field, -1, axis_dim)) * (
        second_field - shifted(second_field, -1, axis_dim)
    )


def face_to_cells(face_sens, axis_dim):
    return 0.5 * (face_sens + shifted(face_sens, 1, axis_dim))


def to_lines_y(stacked):
    partial_move = lax.all_to_all(stacked, "narrow", split_axis=2, concat_axis=1, tiled=True)
    return lax.all_to_all(partial_move, "wide", split_axis=2, concat_axis=1, tiled=True)


def to_lines_x(stacked):
    partial_move = lax.all_to_all(stacked, "wide", split_axis=1, concat_axis=2, tiled=True)
    return lax.all_to_all(partial_move, "narrow", split_axis=1, concat_axis=2, tiled=True)


def local(
    source,
    pressure_start,
    trans_x,
    trans_y,
    trans_z,
    storage,
    adjoint_seed,
    comp_cell,
    comp_well,
    comp_count,
    well_slot,
):
    row_count, line_width, layer_count = source.shape
    devices = lax.axis_size("wide") * lax.axis_size("narrow")
    local_shape = source.shape
    global_row = (
        lax.broadcasted_iota(jnp.int32, local_shape, 0)
        + lax.axis_index(("wide", "narrow")) * row_count
    )
    open_x = jnp.where(
        lax.broadcasted_iota(jnp.int32, local_shape, 1) < line_width - 1, trans_x, 0.0
    )
    open_y = jnp.where(global_row < row_count * devices - 1, trans_y, 0.0)
    open_z = jnp.where(
        lax.broadcasted_iota(jnp.int32, local_shape, 2) < layer_count - 1, trans_z, 0.0
    )
    moved = to_lines_y(jnp.stack([source, pressure_start, open_y, open_z, storage]))
    source_y = moved[0]
    start_y = moved[1]
    open_y_y = moved[2]
    open_z_y = moved[3]
    storage_y = moved[4]
    factor_x = factor_lines(open_x, storage, 1)
    factor_y = factor_lines(open_y_y, storage_y, 0)
    pressure_y = start_y
    states = []
    for iteration in range(ITERS):
        rest_y = (
            source_y - divergence(pressure_y, open_y_y, 0) - divergence(pressure_y, open_z_y, 2)
        )
        middle_field = solve_lines(factor_x, to_lines_x(rest_y[None])[0], 1)
        rest_x = source - divergence(middle_field, open_x, 1) - divergence(middle_field, open_z, 2)
        updated_y = solve_lines(factor_y, to_lines_y(rest_x[None])[0], 0)
        states.append((pressure_y, middle_field, updated_y))
        pressure_y = updated_y

    def y_terms(early_adj, start_state_y, face_y, face_zy):
        early_y = to_lines_y(early_adj[None])[0]
        face_y = face_y - face_product(early_y, start_state_y, 0)
        face_zy = face_zy - face_product(early_y, start_state_y, 2)
        back_next = -(divergence(early_y, open_y_y, 0) + divergence(early_y, open_z_y, 2))
        return (face_y, face_zy, back_next)

    back_y = to_lines_y(adjoint_seed[None])[0]
    grad_source = jnp.zeros(local_shape, jnp.float32)
    face_x = jnp.zeros(local_shape, jnp.float32)
    face_zx = jnp.zeros(local_shape, jnp.float32)
    face_y = jnp.zeros(back_y.shape, jnp.float32)
    face_zy = jnp.zeros(back_y.shape, jnp.float32)
    for iteration in reversed(range(ITERS)):
        start_state_y, middle_field, updated_y = states[iteration]
        late_y = solve_lines(factor_y, back_y, 0)
        late_adj = to_lines_x(late_y[None])[0]
        early_adj = solve_lines(
            factor_x, -(divergence(late_adj, open_x, 1) + divergence(late_adj, open_z, 2)), 1
        )
        grad_source = grad_source + late_adj + early_adj
        face_x = face_x - face_product(late_adj + early_adj, middle_field, 1)
        face_zx = face_zx - face_product(late_adj, middle_field, 2)
        face_y = face_y - face_product(late_y, updated_y, 0)
        if iteration > 0:
            face_y, face_zy, back_y = y_terms(early_adj, start_state_y, face_y, face_zy)
        else:
            face_y, face_zy, back_y = y_terms(early_adj, start_state_y, face_y, face_zy)
    cell_y = face_to_cells(face_y * open_y_y, 0) + face_to_cells(face_zy * open_z_y, 2)
    cell_sens = (
        to_lines_x(cell_y[None])[0]
        + face_to_cells(face_x * open_x, 1)
        + face_to_cells(face_zx * open_z, 2)
    )
    flattened = cell_sens.reshape(row_count, line_width * layer_count)
    picked = jnp.take_along_axis(flattened, comp_cell, axis=1)
    live_mask = lax.broadcasted_iota(jnp.int32, comp_cell.shape, 1) < comp_count[:, None]
    picked = jnp.where(live_mask, picked, 0.0)
    slot_ids = well_slot[comp_well]
    partial_sums = jax.ops.segment_sum(
        picked.reshape(-1), slot_ids.reshape(-1), num_segments=well_slot.shape[0]
    )
    well_sens = lax.psum_scatter(partial_sums, ("wide", "narrow"), scatter_dimension=0, tiled=True)
    return (grad_source, well_sens)


def solution(mesh):
    placed = (
        P(("wide", "narrow"), None, None),
        P(("wide", "narrow"), None, None),
        P(("wide", "narrow"), None, None),
        P(("wide", "narrow"), None, None),
        P(("wide", "narrow"), None, None),
        P(("wide", "narrow"), None, None),
        P(("wide", "narrow"), None, None),
        P(("wide", "narrow"), None),
        P(("wide", "narrow"), None),
        P(("wide", "narrow")),
        P(),
    )
    return jax.shard_map(
        local,
        mesh=mesh,
        in_specs=placed,
        out_specs=(P(("wide", "narrow"), None, None), P(("wide", "narrow"))),
        check_vma=False,
    )
```

profile of v0, /device:TPU:1, one launch (start us, length us, event | category | flops | bytes accessed | tf_op | source)
XLA Modules:
  0.0 1049.2 jit_solution(7139222909606856113)
XLA Ops:
  11.7 40.5 %all_to_all.297 = f32[5,1,512,128]{3,1,0,2:T(1,128)S(1)} all-to-all(f32[5,1,512,128]{3,1,0,2:T(1,128)S(1)} %copy.53), channel_id=1, replica_groups=mesh['wide'=32,'narrow'=16] {'narrow'}, dimensions={2} | all-to-all | bytes 2621440 | tf_op jit(solution)/shard_map/all_to_all | solution.py:72
  53.0 80.8 %all_to_all.298 = f32[5,16,32,128]{3,1,0,2:T(8,128)S(1)} all-to-all(f32[5,16,32,128]{3,1,0,2:T(8,128)S(1)} %copy.55), channel_id=1, replica_groups=mesh['wide'=32,'narrow'=16] {'wide'}, dimensions={2} | all-to-all | bytes 2621440 | tf_op jit(solution)/shard_map/all_to_all | solution.py:73
  136.1 8.5 all-to-all-start.10
  144.6 18.6 %all-to-all-done.10 = f32[1,512,1,128]{3,2,0,1:T(1,128)S(1)} async-done(((f32[1,512,1,128]{3,2,0,1:T(1,128)}), f32[1,512,1,128]{3,2,0,1:T(1,128)S(1)}, u32[]{:S(2)}, u32[]{:S(2)}) %all-to-all-start.10) | async-done | bytes 262176 | tf_op jit(solution)/shard_map/all_to_all | solution.py:77
  164.0 7.6 all-to-all-start.11
  173.4 7.7 all-to-all-done.11
  181.1 4.2 all-to-all-start
  196.5 6.9 all-to-all-start.12
  203.4 1.8 copy.52
  205.2 7.1 all-to-all-done.12
  213.0 7.6 all-to-all-start.1
  220.6 1.8 copy.66
  222.4 18.4 %all-to-all-done.1 = f32[1,16,32,128]{3,1,0,2:T(8,128)S(1)} async-done(((f32[1,16,32,128]{3,1,0,2:T(8,128)}), f32[1,16,32,128]{3,1,0,2:T(8,128)S(1)}, u32[]{:S(2)}, u32[]{:S(2)}) %all-to-all-start.1) | async-done | bytes 262176 | tf_op jit(solution)/shard_map/all_to_all | solution.py:73
  240.8 6.7 all-to-all-start.13
  250.0 15.5 %all-to-all-done.13 = f32[1,16,32,128]{3,1,0,2:T(8,128)} async-done(((f32[1,16,32,128]{3,1,0,2:T(8,128)}), f32[1,16,32,128]{3,1,0,2:T(8,128)}, u32[]{:S(2)}, u32[]{:S(2)}) %all-to-all-start.13) | async-done | bytes 262176 | tf_op jit(solution)/shard_map/all_to_all | solution.py:73
  277.6 7.4 all-to-all-start.4
  286.9 18.3 %all-to-all-done.4 = f32[1,512,1,128]{3,2,0,1:T(1,128)} async-done(((f32[1,512,1,128]{3,2,0,1:T(1,128)}), f32[1,512,1,128]{3,2,0,1:T(1,128)}, u32[]{:S(2)}, u32[]{:S(2)}) %all-to-all-start.4) | async-done | bytes 262176 | tf_op jit(solution)/shard_map/all_to_all | solution.py:77
  305.2 6.3 all-to-all-start.14
  311.5 1.7 copy.58
  313.3 18.4 %all-to-all-done.14 = f32[1,512,1,128]{3,2,0,1:T(1,128)S(1)} async-done(((f32[1,512,1,128]{3,2,0,1:T(1,128)}), f32[1,512,1,128]{3,2,0,1:T(1,128)S(1)}, u32[]{:S(2)}, u32[]{:S(2)}) %all-to-all-start.14) | async-done | bytes 262176 | tf_op jit(solution)/shard_map/all_to_all | solution.py:77
  332.4 8.4 all-to-all-start.5
  340.8 1.7 copy.68
  342.5 7.5 all-to-all-done.5
  350.0 4.4 all-to-all-start.15
  356.6 1.9 fusion.61
  358.5 4.8 all-to-all-done.15
  373.8 4.3 all-to-all-start.6
  380.1 7.1 all-to-all-done.6
  387.2 3.5 all-to-all-start.16
  390.7 1.8 copy.60
  392.6 7.1 all-to-all-done.16
  400.3 8.9 all-to-all-start.7
  409.2 1.8 copy.70
  411.1 18.4 %all-to-all-done.7 = f32[1,16,32,128]{3,1,0,2:T(8,128)S(1)} async-done(((f32[1,16,32,128]{3,1,0,2:T(8,128)}), f32[1,16,32,128]{3,1,0,2:T(8,128)S(1)}, u32[]{:S(2)}, u32[]{:S(2)}) %all-to-all-start.7) | async-done | bytes 262176 | tf_op jit(solution)/shard_map/all_to_all | solution.py:73
  429.5 6.9 all-to-all-start.17
  438.0 16.0 %all-to-all-done.17 = f32[1,16,32,128]{3,1,0,2:T(8,128)} async-done(((f32[1,16,32,128]{3,1,0,2:T(8,128)}), f32[1,16,32,128]{3,1,0,2:T(8,128)}, u32[]{:S(2)}, u32[]{:S(2)}) %all-to-all-start.17) | async-done | bytes 262176 | tf_op jit(solution)/shard_map/all_to_all | solution.py:73
  455.1 1.4 multiply_subtract_fusion.7
  466.5 27.8 %all_to_all.299 = f32[1,512,1,128]{3,2,0,1:T(1,128)S(1)} all-to-all(f32[1,512,1,128]{3,2,0,1:T(1,128)S(1)} %bitcast.213), channel_id=1, replica_groups=mesh['wide'=32,'narrow'=16] {'wide'}, dimensions={1} | all-to-all | bytes 524288 | tf_op jit(solution)/shard_map/all_to_all | solution.py:77
  494.4 18.0 %all_to_all.300 = f32[1,16,32,128]{3,2,0,1:T(8,128)S(1)} all-to-all(f32[1,16,32,128]{3,2,0,1:T(8,128)S(1)} %copy.62), channel_id=1, replica_groups=mesh['wide'=32,'narrow'=16] {'narrow'}, dimensions={1} | all-to-all | bytes 524288 | tf_op jit(solution)/shard_map/all_to_all | solution.py:78
  520.2 13.3 %all_to_all.301 = f32[1,1,512,128]{3,1,0,2:T(1,128)S(1)} all-to-all(f32[1,1,512,128]{3,1,0,2:T(1,128)S(1)} %bitcast.220), channel_id=1, replica_groups=mesh['wide'=32,'narrow'=16] {'narrow'}, dimensions={2} | all-to-all | bytes 524288 | tf_op jit(solution)/shard_map/all_to_all | solution.py:72
  534.3 5.9 all-to-all-start.19
  541.7 1.7 slice.1484
  543.3 17.1 %all-to-all-done.19 = f32[1,16,32,128]{3,1,0,2:T(8,128)S(1)} async-done(((f32[1,16,32,128]{3,1,0,2:T(8,128)}), f32[1,16,32,128]{3,1,0,2:T(8,128)S(1)}, u32[]{:S(2)}, u32[]{:S(2)}) %all-to-all-start.19) | async-done | bytes 262176 | tf_op jit(solution)/shard_map/all_to_all | solution.py:73
  562.8 26.7 %all_to_all.302 = f32[1,512,1,128]{3,2,0,1:T(1,128)S(1)} all-to-all(f32[1,512,1,128]{3,2,0,1:T(1,128)S(1)} %bitcast.234), channel_id=1, replica_groups=mesh['wide'=32,'narrow'=16] {'wide'}, dimensions={1} | all-to-all | bytes 524288 | tf_op jit(solution)/shard_map/all_to_all | solution.py:77
  590.2 7.3 all-to-all-start.21
  600.4 7.0 all-to-all-done.21
  608.4 1.5 scatter_custom_fusion
  609.9 431.1 %all-reduce.292.cloned.1.call-done = f32[20480]{0:T(1024)} async-done(((f32[20480]{0:T(1024)}), f32[20480]{0:T(1024)}) %all-reduce.292.cloned.1.call-update) | async-done | bytes 81936
  (565 shorter events, 82.2 us)
Async XLA Ops:
  7.2 591.1 %copy-start = (s32[20480]{0:T(1024)S(1)}, s32[20480]{0:T(1024)}, u32[]{:S(2)}) copy-start(s32[20480]{0:T(1024)} %param.21) | copy-start | bytes 245764
  7.2 3.0 copy-start.31
  7.2 3.1 copy-start.99
  134.1 151.1 %copy-start.5 = (f32[1,32,16,1,128]{4,2,1,3,0:T(8,128)}, f32[1,32,16,1,128]{4,2,1,3,0:T(8,128)S(1)}, u32[]{:S(2)}) copy-start(f32[1,32,16,1,128]{4,2,1,3,0:T(8,128)S(1)} %get-tuple-element.125) | copy-start | bytes 786436
  135.2 36.4 %copy-start.153 = (f32[1,512,128]{2,1,0:T(8,128)S(1)}, f32[1,512,128]{2,1,0:T(8,128)}, u32[]{:S(2)}) copy-start(f32[1,512,128]{2,1,0:T(8,128)} %param.13) | copy-start | bytes 786436
  136.1 27.1 %all-to-all-start.10 = ((f32[1,512,1,128]{3,2,0,1:T(1,128)}), f32[1,512,1,128]{3,2,0,1:T(1,128)S(1)}, u32[]{:S(2)}, u32[]{:S(2)}) async-start(f32[1,512,1,128]{3,2,0,1:T(1,128)} %bitcast.44), calls=%async_computation.10 | async-start | bytes 524288 | tf_op jit(solution)/shard_map/all_to_all | solution.py:77
  164.0 17.1 %all-to-all-start.11 = ((f32[1,16,32,128]{3,2,0,1:T(8,128)}), f32[1,16,32,128]{3,2,0,1:T(8,128)S(1)}, u32[]{:S(2)}, u32[]{:S(2)}) async-start(f32[1,16,32,128]{3,2,0,1:T(8,128)} %copy.64), calls=%async_computation.11 | async-start | bytes 524288 | tf_op jit(solution)/shard_map/all_to_all | solution.py:78
  181.1 15.4 %all-to-all-start = ((f32[1,1,512,128]{3,1,0,2:T(1,128)}), f32[1,1,512,128]{3,1,0,2:T(1,128)}, u32[]{:S(2)}, u32[]{:S(2)}) async-start(f32[1,1,512,128]{3,1,0,2:T(1,128)} %bitcast), calls=%async_computation | async-start | bytes 524288 | tf_op jit(solution)/shard_map/all_to_all | solution.py:72
  188.4 177.7 %copy-start.1 = (f32[1,512,128]{2,1,0:T(8,128)}, f32[1,512,128]{2,1,0:T(8,128)S(1)}, u32[]{:S(2)}) copy-start(f32[1,512,128]{2,1,0:T(8,128)S(1)} %get-tuple-element.68) | copy-start | bytes 786436
  188.4 177.7 %copy-start.3 = (f32[1,512,128]{2,1,0:T(8,128)}, f32[1,512,128]{2,1,0:T(8,128)S(1)}, u32[]{:S(2)}) copy-start(f32[1,512,128]{2,1,0:T(8,128)S(1)} %get-tuple-element.70) | copy-start | bytes 786436
  188.9 177.4 %copy-start.8 = (f32[1,512,128]{2,1,0:T(8,128)}, f32[1,512,128]{2,1,0:T(8,128)S(1)}, u32[]{:S(2)}) copy-start(f32[1,512,128]{2,1,0:T(8,128)S(1)} %get-tuple-element.63) | copy-start | bytes 786436
  196.5 15.8 %all-to-all-start.12 = ((f32[1,1,512,128]{3,1,0,2:T(1,128)}), f32[1,1,512,128]{3,1,0,2:T(1,128)S(1)}, u32[]{:S(2)}, u32[]{:S(2)}) async-start(f32[1,1,512,128]{3,1,0,2:T(1,128)} %bitcast.244), calls=%async_computation.12 | async-start | bytes 524288 | tf_op jit(solution)/shard_map/all_to_all | solution.py:72
  213.0 27.8 %all-to-all-start.1 = ((f32[1,16,32,128]{3,1,0,2:T(8,128)}), f32[1,16,32,128]{3,1,0,2:T(8,128)S(1)}, u32[]{:S(2)}, u32[]{:S(2)}) async-start(f32[1,16,32,128]{3,1,0,2:T(8,128)} %copy.52), calls=%async_computation.1 | async-start | bytes 524288 | tf_op jit(solution)/shard_map/all_to_all | solution.py:73
  240.8 24.8 %all-to-all-start.13 = ((f32[1,16,32,128]{3,1,0,2:T(8,128)}), f32[1,16,32,128]{3,1,0,2:T(8,128)}, u32[]{:S(2)}, u32[]{:S(2)}) async-start(f32[1,16,32,128]{3,1,0,2:T(8,128)} %copy.66), calls=%async_computation.13 | async-start | bytes 524288 | tf_op jit(solution)/shard_map/all_to_all | solution.py:73
  247.5 1.7 copy-start.98
  268.0 1.6 copy-start.70
  268.0 1.6 copy-start.71
  277.6 27.6 %all-to-all-start.4 = ((f32[1,512,1,128]{3,2,0,1:T(1,128)}), f32[1,512,1,128]{3,2,0,1:T(1,128)}, u32[]{:S(2)}, u32[]{:S(2)}) async-start(f32[1,512,1,128]{3,2,0,1:T(1,128)} %bitcast.212), calls=%async_computation.4 | async-start | bytes 524288 | tf_op jit(solution)/shard_map/all_to_all | solution.py:77
  305.2 26.5 %all-to-all-start.14 = ((f32[1,512,1,128]{3,2,0,1:T(1,128)}), f32[1,512,1,128]{3,2,0,1:T(1,128)S(1)}, u32[]{:S(2)}, u32[]{:S(2)}) async-start(f32[1,512,1,128]{3,2,0,1:T(1,128)} %bitcast.243), calls=%async_computation.14 | async-start | bytes 524288 | tf_op jit(solution)/shard_map/all_to_all | solution.py:77
  332.4 17.7 %all-to-all-start.5 = ((f32[1,16,32,128]{3,2,0,1:T(8,128)}), f32[1,16,32,128]{3,2,0,1:T(8,128)S(1)}, u32[]{:S(2)}, u32[]{:S(2)}) async-start(f32[1,16,32,128]{3,2,0,1:T(8,128)} %copy.58), calls=%async_computation.5 | async-start | bytes 524288 | tf_op jit(solution)/shard_map/all_to_all | solution.py:78
  350.0 13.3 %all-to-all-start.15 = ((f32[1,16,32,128]{3,2,0,1:T(8,128)}), f32[1,16,32,128]{3,2,0,1:T(8,128)}, u32[]{:S(2)}, u32[]{:S(2)}) async-start(f32[1,16,32,128]{3,2,0,1:T(8,128)} %copy.68), calls=%async_computation.15 | async-start | bytes 524288 | tf_op jit(solution)/shard_map/all_to_all | solution.py:78
  354.6 2.0 copy-start.114
  373.8 4.5 copy-start.32
  373.8 13.4 %all-to-all-start.6 = ((f32[1,1,512,128]{3,1,0,2:T(1,128)}), f32[1,1,512,128]{3,1,0,2:T(1,128)}, u32[]{:S(2)}, u32[]{:S(2)}) async-start(f32[1,1,512,128]{3,1,0,2:T(1,128)} %bitcast.232), calls=%async_computation.6 | async-start | bytes 524288 | tf_op jit(solution)/shard_map/all_to_all | solution.py:72
  378.2 1.9 copy-start.102
  387.2 12.4 %all-to-all-start.16 = ((f32[1,1,512,128]{3,1,0,2:T(1,128)}), f32[1,1,512,128]{3,1,0,2:T(1,128)S(1)}, u32[]{:S(2)}, u32[]{:S(2)}) async-start(f32[1,1,512,128]{3,1,0,2:T(1,128)} %bitcast.245), calls=%async_computation.16 | async-start | bytes 524288 | tf_op jit(solution)/shard_map/all_to_all | solution.py:72
  392.6 43.9 %copy-start.6 = (f32[1,32,16,1,128]{4,2,1,3,0:T(8,128)S(1)}, f32[1,32,16,1,128]{4,2,1,3,0:T(8,128)}, u32[]{:S(2)}) copy-start(f32[1,32,16,1,128]{4,2,1,3,0:T(8,128)} %copy-done.5) | copy-start | bytes 786436
  400.3 29.1 %all-to-all-start.7 = ((f32[1,16,32,128]{3,1,0,2:T(8,128)}), f32[1,16,32,128]{3,1,0,2:T(8,128)S(1)}, u32[]{:S(2)}, u32[]{:S(2)}) async-start(f32[1,16,32,128]{3,1,0,2:T(8,128)} %copy.60), calls=%async_computation.7 | async-start | bytes 524288 | tf_op jit(solution)/shard_map/all_to_all | solution.py:73
  429.5 24.6 %all-to-all-start.17 = ((f32[1,16,32,128]{3,1,0,2:T(8,128)}), f32[1,16,32,128]{3,1,0,2:T(8,128)}, u32[]{:S(2)}, u32[]{:S(2)}) async-start(f32[1,16,32,128]{3,1,0,2:T(8,128)} %copy.70), calls=%async_computation.17 | async-start | bytes 524288 | tf_op jit(solution)/shard_map/all_to_all | solution.py:73
  466.5 27.8 %copy-start.73 = (f32[512,1,128]{2,0,1:T(8,128)}, f32[512,1,128]{2,0,1:T(8,128)S(1)}, u32[]{:S(2)}) copy-start(f32[512,1,128]{2,0,1:T(8,128)S(1)} %get-tuple-element.117) | copy-start | bytes 786436
  466.5 46.1 %copy-start.33 = (f32[1,512,128]{2,1,0:T(8,128)S(1)}, f32[1,512,128]{2,1,0:T(8,128)}, u32[]{:S(2)}) copy-start(f32[1,512,128]{2,1,0:T(8,128)} %param.15) | copy-start | bytes 786436
  466.5 46.1 %copy-start.112 = (f32[1,512,127]{2,1,0:T(8,128)S(1)}, f32[1,512,127]{2,1,0:T(8,128)}, u32[]{:S(2)}) copy-start(f32[1,512,127]{2,1,0:T(8,128)} %copy-done.111) | copy-start | bytes 780292
  466.5 46.1 %copy-start.115 = (f32[1,512,127]{2,1,0:T(8,128)S(1)}, f32[1,512,127]{2,1,0:T(8,128)}, u32[]{:S(2)}) copy-start(f32[1,512,127]{2,1,0:T(8,128)} %copy-done.114) | copy-start | bytes 780292
  466.5 46.1 %copy-start.117 = (f32[1,512,127]{2,1,0:T(8,128)S(1)}, f32[1,512,127]{2,1,0:T(8,128)}, u32[]{:S(2)}) copy-start(f32[1,512,127]{2,1,0:T(8,128)} %copy-done.116) | copy-start | bytes 780292
  519.5 20.7 %copy-start.72 = (f32[512,1,128]{2,0,1:T(8,128)S(1)}, f32[512,1,128]{2,0,1:T(8,128)}, u32[]{:S(2)}) copy-start(f32[512,1,128]{2,0,1:T(8,128)} %get-tuple-element.121) | copy-start | bytes 786436
  519.5 21.5 %copy-start.74 = (f32[512,1,128]{2,0,1:T(8,128)S(1)}, f32[512,1,128]{2,0,1:T(8,128)}, u32[]{:S(2)}) copy-start(f32[512,1,128]{2,0,1:T(8,128)} %copy-done.73) | copy-start | bytes 786436
  534.3 26.1 %all-to-all-start.19 = ((f32[1,16,32,128]{3,1,0,2:T(8,128)}), f32[1,16,32,128]{3,1,0,2:T(8,128)S(1)}, u32[]{:S(2)}, u32[]{:S(2)}) async-start(f32[1,16,32,128]{3,1,0,2:T(8,128)} %copy.72), calls=%async_computation.19 | async-start | bytes 524288 | tf_op jit(solution)/shard_map/all_to_all | solution.py:73
  540.2 20.4 %copy-start.7 = (f32[1,32,16,1,128]{4,2,1,3,0:T(8,128)S(1)}, f32[1,32,16,1,128]{4,2,1,3,0:T(8,128)}, u32[]{:S(2)}) copy-start(f32[1,32,16,1,128]{4,2,1,3,0:T(8,128)} %copy-done.5) | copy-start | bytes 786436
  560.7 1.5 copy-start.146
  560.7 1.6 copy-start.147
  562.6 35.1 %copy-start.155 = (s32[1,64]{1,0:T(1,128)S(1)}, s32[1,64]{1,0:T(1,128)}, u32[]{:S(2)}) copy-start(s32[1,64]{1,0:T(1,128)} %param.19) | copy-start | bytes 772
  562.7 36.4 %copy-start.154 = (s32[1,64]{1,0:T(1,128)S(1)}, s32[1,64]{1,0:T(1,128)}, u32[]{:S(2)}) copy-start(s32[1,64]{1,0:T(1,128)} %param.18) | copy-start | bytes 772
  562.7 36.4 %copy-start.105 = (f32[1,512,128]{2,1,0:T(8,128)S(1)}, f32[1,512,128]{2,1,0:T(8,128)}, u32[]{:S(2)}) copy-start(f32[1,512,128]{2,1,0:T(8,128)} %copy-done.104) | copy-start | bytes 786436
  562.7 36.4 %copy-start.113 = (f32[1,512,128]{2,1,0:T(8,128)S(1)}, f32[1,512,128]{2,1,0:T(8,128)}, u32[]{:S(2)}) copy-start(f32[1,512,128]{2,1,0:T(8,128)} %get-tuple-element.119) | copy-start | bytes 786436
  590.2 17.2 %all-to-all-start.21 = ((f32[1,16,32,128]{3,2,0,1:T(8,128)}), f32[1,16,32,128]{3,2,0,1:T(8,128)S(1)}, u32[]{:S(2)}, u32[]{:S(2)}) async-start(f32[1,16,32,128]{3,2,0,1:T(8,128)} %copy.74), calls=%async_computation.21 | async-start | bytes 524288 | tf_op jit(solution)/shard_map/all_to_all | solution.py:78
  597.6 443.5 %all-reduce.292.cloned.1.call-start = ((), (), s32[]{:S(2)}) async-start(), calls=%async_computation.22 | async-start | bytes 163840
  598.3 1.6 copy-start.97
  600.3 7.2 copy-start.120
  (125 other events, 122.2 us)
Sparse Core Ops, SparseCore 0:
  610.0 430.9 all-reduce.291
where the time goes:
time: 1050 us
  waiting for transfers between devices  620 us (59%)
  blocking collectives  207 us (20%)
  starting transfers between devices  105 us (10%)
  local copies, waits for them, and re-layouts  69.3 us (7%)
  other arithmetic  30.1 us (3%)
  between operations  17.6 us (2%)
    unnamed x2, waiting for transfers between devices  431 us
    all_to_all x5, waiting for transfers between devices, to_lines_y(): lax.all_to_all(partial_move, 'wide', split_axis=2, concat_axis=1, tiled=T...  85.4 us
    all_to_all x1, blocking collectives, to_lines_y(): lax.all_to_all(partial_move, 'wide', split_axis=2, concat_axis=1, tiled=T...  80.8 us
    all_to_all x3, waiting for transfers between devices, to_lines_x(): lax.all_to_all(stacked, 'wide', split_axis=1, concat_axis=2, tiled=True)  55.2 us
    all_to_all x2, blocking collectives, to_lines_x(): lax.all_to_all(stacked, 'wide', split_axis=1, concat_axis=2, tiled=True)  54.4 us
    all_to_all x2, blocking collectives, to_lines_y(): lax.all_to_all(stacked, 'narrow', split_axis=2, concat_axis=1, tiled=True)  53.8 us
    all_to_all x5, starting transfers between devices, to_lines_y(): lax.all_to_all(partial_move, 'wide', split_axis=2, concat_axis=1, tiled=T...  35.9 us
    unnamed x315, local copies, waits for them, and re-layouts  35.8 us
  transfers between devices with their start and end apart: 17, of which 16 were waited for; matrix products, arithmetic and copies ran while one was open for 3% of the time, Pallas kernels for 0%

commit v1 on v0

v1 whole, which is shorter than its diff:
```python
import functools

import jax
import jax.numpy as jnp
from jax import lax
from jax.experimental import pallas as pl
from jax.experimental.pallas import tpu as pltpu
from jax.sharding import PartitionSpec as P

MESH = pl.DeviceIdType.MESH
HIGHEST = lax.Precision.HIGHEST
PAD = 8

(
    T_TY, T_ST, T_SEED, T_B0, T_RW, T_B1, T_LATE1, T_P1, T_W, T_P2,
    T_PNEXT, T_FLUX, T_CELL_P, T_CELL_N, T_SLOT, T_VAL, T_MSG_P, T_MSG_N,
    T_COEF, T_S0, T_S1, T_S2, T_S3, T_R0, T_R1, T_R2, T_R3, T_PART, T_COUNT,
) = range(29)
L_SRC, L_P0, L_TX, L_TY, L_TZ, L_ST, L_COUNT = range(7)


def levels_of(extent):
    return max(1, (extent - 1).bit_length())


def kernel(
    nw, nn, nx, nk, cap, owned,
    source, pressure, trans_x, trans_y, trans_z, storage, seed, cell, well, count, slots,
    grad_out, well_out,
    src, p0, tx, ty, tz, st, p_next, flux, f_prev,
    ty_y, st_y, seed_y, b0_y, rw_y, b1_y,
    inv_y, m_y, ga_y, gb_y, late1_y, p1_y, w_y, p2_y,
    late1, p1, w_x, p2, b0, b1, rw, u0, u1, early1, early0, late0, sum0, sum1,
    gain_l, gain_r, inv_x, mid_x, ba, bb, bc,
    coef_s, coef_r, to_s, to_r, re_s, re_r,
    ia, ib, ic, pk_l, pk_r, pk_inv, tau, kap, f0s,
    cell_s, cell_r, pick_rows, onehot, lane_mask, gathered, own_v, msg_p, msg_n, msg_r,
    slot_s, slot_r, val_s, val_r, part_s, part_r,
    send_sem, recv_sem, load_sem,
):
    wi, ni = lax.axis_index("wide"), lax.axis_index("narrow")
    rows = nw * nn
    row = wi * nn + ni
    nxt, prv = lax.rem(row + 1, rows), lax.rem(row + rows - 1, rows)
    next_dev = {"wide": nxt // nn, "narrow": lax.rem(nxt, nn)}
    prev_dev = {"wide": prv // nn, "narrow": lax.rem(prv, nn)}
    xc = nx // nn
    lev, pad_x = levels_of(nx), nx // 2
    lev_w, pad_w = levels_of(nw), max(PAD, nw // 2)
    bl = min(64, nx)
    blocks = nx // bl

    barrier = pltpu.get_barrier_semaphore()

    def greet_narrow(k, c):
        pl.semaphore_signal(barrier, inc=1, device_id={"narrow": lax.rem(ni + k, nn)}, device_id_type=MESH)
        return c

    def greet_wide(k, c):
        pl.semaphore_signal(barrier, inc=1, device_id={"wide": lax.rem(wi + k, nw)}, device_id_type=MESH)
        return c

    pl.semaphore_signal(barrier, inc=1, device_id=next_dev, device_id_type=MESH)
    pl.semaphore_signal(barrier, inc=1, device_id=prev_dev, device_id_type=MESH)
    lax.fori_loop(1, nn, greet_narrow, 0)
    lax.fori_loop(1, nw, greet_wide, 0)

    loads = [
        pltpu.make_async_copy(storage, st, load_sem.at[L_ST]),
        pltpu.make_async_copy(trans_x, tx.at[pl.ds(PAD, nx)], load_sem.at[L_TX]),
        pltpu.make_async_copy(trans_y, ty, load_sem.at[L_TY]),
        pltpu.make_async_copy(pressure, p0, load_sem.at[L_P0]),
        pltpu.make_async_copy(source, src, load_sem.at[L_SRC]),
        pltpu.make_async_copy(trans_z, tz, load_sem.at[L_TZ]),
    ]
    for one in loads:
        one.start()

    def remote(from_ref, to_ref, number, device):
        return pltpu.make_async_remote_copy(
            src_ref=from_ref, dst_ref=to_ref, send_sem=send_sem.at[number], recv_sem=recv_sem.at[number],
            device_id=device, device_id_type=MESH,
        )

    def spread_narrow(number, from_of, to_ref):
        def body(k, c):
            j = lax.rem(ni + k, nn)
            remote(from_of(j), to_ref, number, {"narrow": j}).start()
            return c

        lax.fori_loop(1, nn, body, 0)
        pltpu.make_async_copy(from_of(ni), to_ref, recv_sem.at[number]).start()

    def spread_wide(number, from_ref, to_ref):
        def body(k, c):
            j = lax.rem(wi + k, nw)
            remote(from_ref.at[j], to_ref.at[wi], number, {"wide": j}).start()
            return c

        lax.fori_loop(1, nw, body, 0)
        pltpu.make_async_copy(from_ref.at[wi], to_ref.at[wi], recv_sem.at[number]).start()

    def chunk(ref):
        return lambda j: ref.at[pl.ds(pl.multiple_of(j * xc, xc), xc)]

    def to_y(number, from_ref, to_ref):
        spread_narrow(number, chunk(from_ref), to_ref.at[ni])

    def to_x(number, from_ref, to_ref):
        spread_narrow(number, lambda j: from_ref.at[j], to_ref.at[pl.ds(pl.multiple_of(PAD + ni * xc, PAD), xc)])

    def arrived(number, ref):
        pltpu.make_async_copy(ref, ref, recv_sem.at[number]).wait()

    def sent(number, ref):
        pltpu.make_async_copy(ref, ref, send_sem.at[number]).wait()

    def inner(ref):
        return ref.at[pl.ds(PAD, nx)]

    zeros_pad = jnp.zeros((PAD, nk), jnp.float32)
    for ref in (tx, late1, p1, w_x, p2, u0, u1, early1, early0, late0, sum0, sum1):
        ref[0:PAD, :] = zeros_pad
        ref[PAD + nx : 2 * PAD + nx, :] = zeros_pad
    zeros_x = jnp.zeros((pad_x, nk), jnp.float32)
    for ref in (ba, bb, bc):
        ref[0:pad_x, :] = zeros_x
        ref[pad_x + nx : 2 * pad_x + nx, :] = zeros_x
    zeros_w = jnp.zeros((pad_w, nk), jnp.float32)
    for ref in (ia, ib, ic):
        ref[0:pad_w, :] = zeros_w
        ref[pad_w + nw : 2 * pad_w + nw, :] = zeros_w
    for ref in (own_v, msg_p, msg_n):
        ref[...] = jnp.zeros_like(ref)

    cell_s[...] = jnp.zeros_like(cell_s)
    cell_s[0:1, 0:cap] = cell[...].astype(jnp.float32)

    def column(line):
        eye = lax.broadcasted_iota(jnp.int32, (cap, nk), 0) == lax.broadcasted_iota(jnp.int32, (cap, nk), 1)
        return jnp.sum(jnp.where(eye, jnp.broadcast_to(line, (cap, nk)), 0.0), axis=1, keepdims=True)

    def lanes_to_line(values):
        ones = jnp.ones((8, nk), jnp.float32)
        return lax.dot_general(
            ones, values, (((1,), (1,)), ((), ())), precision=HIGHEST, preferred_element_type=jnp.float32
        )[0:1, :]

    pick_rows[...] = jnp.zeros_like(pick_rows)
    pick_rows[0:1, 0:cap] = well[...].astype(jnp.float32)
    well_col = column(pick_rows[0:1, :])
    slot_rows = slots.shape[0]
    high = jnp.floor(well_col * (1.0 / nk))
    low = well_col - high * nk
    table_hot = jnp.where(
        jnp.broadcast_to(high, (cap, slot_rows)) == lax.broadcasted_iota(jnp.int32, (cap, slot_rows), 1).astype(jnp.float32),
        1.0, 0.0,
    )
    table = jnp.dot(table_hot, slots[...].astype(jnp.float32), precision=HIGHEST, preferred_element_type=jnp.float32)
    table = jnp.where(
        jnp.broadcast_to(low, (cap, nk)) == lax.broadcasted_iota(jnp.int32, (cap, nk), 1).astype(jnp.float32), table, 0.0
    )
    live = lax.broadcasted_iota(jnp.int32, (1, cap), 1) < count[0, 0]
    slot_s[...] = jnp.full_like(slot_s, -1.0)
    slot_s[0, 0:1, 0:cap] = jnp.where(live, lanes_to_line(table), -1.0)

    pl.semaphore_wait(barrier, nn - 1 + nw - 1 + 2)

    remote(pressure, p_next, T_PNEXT, prev_dev).start()
    to_y(T_TY, trans_y, ty_y)
    to_y(T_ST, storage, st_y)
    to_y(T_SEED, seed, seed_y)
    remote(cell_s, cell_r.at[1], T_CELL_P, prev_dev).start()
    remote(cell_s, cell_r.at[0], T_CELL_N, next_dev).start()
    spread_narrow(T_SLOT, lambda j: slot_s.at[0], slot_r.at[ni])

    def each_block(body):
        def step(i, c):
            body(pl.multiple_of(i * bl, bl))
            return c

        lax.fori_loop(0, blocks, step, 0)

    def at(ref, o, shift=0):
        return ref[pl.ds(o + shift, bl), :]

    def up(ref, o, shift=0):
        return ref[pl.ds(o + (PAD + shift), bl), :]

    def big(ref, o, shift=0):
        return ref[pl.ds(o + (pad_x + shift), bl), :]

    def next_layer(v):
        return pltpu.roll(v, nk - 1, 1)

    def prev_layer(v):
        return pltpu.roll(v, 1, 1)

    def div_z(v, o):
        f = at(tz, o) * (v - next_layer(v))
        return f - prev_layer(f)

    def div_x(ref, o):
        v = up(ref, o)
        return up(tx, o) * (v - up(ref, o, 1)) - up(tx, o, -1) * (up(ref, o, -1) - v)

    def solve_x(out):
        pair = (ba, bb)
        for level in range(lev):
            stride = 1 << level
            a, b = pair[level % 2], pair[1 - level % 2]

            def body(o):
                v = big(a, o)
                v = v + gain_l[level, pl.ds(o, bl), :] * big(a, o, -stride)
                v = v + gain_r[level, pl.ds(o, bl), :] * big(a, o, stride)
                if level == lev - 1:
                    out[pl.ds(o + PAD, bl), :] = v * at(inv_x, o)
                else:
                    b[pl.ds(o + pad_x, bl), :] = v

            each_block(body)

    def factor_x():
        def begin(o):
            t = up(tx, o)
            bb[pl.ds(o + pad_x, bl), :] = -t
            mid_x[pl.ds(o, bl), :] = at(st, o) + t + up(tx, o, -1)

        each_block(begin)
        pair = (bb, bc)
        for level in range(lev):
            stride = 1 << level
            a, b = pair[level % 2], pair[1 - level % 2]

            def invert(o):
                ba[pl.ds(o + pad_x, bl), :] = 1.0 / at(mid_x, o)

            def body(o):
                ua, ul = big(a, o), big(a, o, -stride)
                left = ul * big(ba, o, -stride)
                right = ua * big(ba, o, stride)
                gain_l[level, pl.ds(o, bl), :] = -left
                gain_r[level, pl.ds(o, bl), :] = -right
                b[pl.ds(o + pad_x, bl), :] = -right * big(a, o, stride)
                mid_x[pl.ds(o, bl), :] = at(mid_x, o) - left * ul - right * ua

            each_block(invert)
            each_block(body)

        def finish(o):
            inv_x[pl.ds(o, bl), :] = 1.0 / at(mid_x, o)

        each_block(finish)

    last = nn - 1

    def factor_y():
        def down(j, carry):
            delta, e = carry
            t = ty_y[j]
            iv = 1.0 / (delta + t)
            m = t * iv
            inv_y[j] = iv
            m_y[j] = m
            ga_y[j] = e
            return st_y[j + 1] + m * delta, m * e

        dee, kappa = lax.fori_loop(0, last, down, (st_y[0], jnp.ones((xc, nk), jnp.float32)))

        def back(i, carry):
            a, b = carry
            j = last - 1 - i
            m = m_y[j]
            a = inv_y[j] * ga_y[j] + m * a
            b = m * b
            ga_y[j] = a
            gb_y[j] = b
            return a, b

        corner, _ = lax.fori_loop(
            0, last, back, (jnp.zeros((xc, nk), jnp.float32), jnp.ones((xc, nk), jnp.float32))
        )
        t_last = jnp.where(wi == nw - 1, 0.0, ty_y[last])
        for number, value in enumerate((dee, kappa, corner, t_last)):
            coef_s[:, number, :] = value

    def reduce_y(rhs, slot):
        def body(j, carry):
            a, f = carry
            v = rhs[j]
            return a + gb_y[j] * v, f + ga_y[j] * v

        a, f = lax.fori_loop(0, last, body, (rhs[last], jnp.zeros((xc, nk), jnp.float32)))
        to_s[slot, :, 0, :] = a
        to_s[slot, :, 1, :] = f

    def inside_y(rhs, out):
        def down(j, c):
            out[j] = c
            return rhs[j + 1] + m_y[j] * c

        lax.fori_loop(0, last, down, rhs[0])

        def back(i, c):
            j = last - 1 - i
            c = inv_y[j] * out[j] + m_y[j] * c
            out[j] = c
            return c

        lax.fori_loop(0, last, back, jnp.zeros((xc, nk), jnp.float32))

    def complete_y(out, slot):
        phi = re_r[slot, :, 0, :]
        sep = re_r[slot, :, 1, :]

        def body(j, c):
            out[j] = out[j] + ga_y[j] * phi + gb_y[j] * sep
            return c

        lax.fori_loop(0, last, body, 0)
        out[last] = sep

    def mid(ref, shift=0):
        return ref[pad_w + shift : pad_w + shift + nw, :]

    def put(ref, value):
        ref[pad_w : pad_w + nw, :] = value

    def factor_sep():
        dee, kappa, corner, t_last = (coef_r[:, number, :] for number in range(4))
        put(ia, t_last)
        t_in = mid(ia, -1)
        tau_v = t_in / (1.0 + t_in * corner)
        tau[...] = tau_v
        kap[...] = kappa
        put(ia, tau_v)
        put(ib, tau_v * kappa)
        middle = dee + mid(ia, 1) + kappa * kappa * tau_v
        upper = -mid(ib, 1)
        for level in range(lev_w):
            stride = 1 << level
            put(ia, 1.0 / middle)
            put(ib, upper)
            lower = mid(ib, -stride)
            left = lower * mid(ia, -stride)
            right = upper * mid(ia, stride)
            pk_l[level] = -left
            pk_r[level] = -right
            middle = middle - left * lower - right * upper
            upper = -right * mid(ib, stride)
        pk_inv[...] = 1.0 / middle

    def solve_sep(slot):
        alpha = to_r[slot, :, 0, :]
        f0 = to_r[slot, :, 1, :]
        tf = tau[...] * f0
        put(ic, tf)
        v = alpha + mid(ic, 1) - kap[...] * tf
        for level in range(lev_w):
            stride = 1 << level
            ref = (ia, ib)[level % 2]
            put(ref, v)
            v = v + pk_l[level] * mid(ref, -stride) + pk_r[level] * mid(ref, stride)
        v = v * pk_inv[...]
        put(ic, v)
        re_s[slot, :, 0, :] = tau[...] * (mid(ic, -1) - f0 - kap[...] * v)
        re_s[slot, :, 1, :] = v

    def prepare_picks():
        for number, line in enumerate((cell_s[0:1, :], cell_r[0], cell_r[1])):
            col = column(line)
            x_of = jnp.floor(col * (1.0 / nk))
            layer = col - x_of * nk
            rows_at = pl.ds(number * cap, cap)
            onehot[rows_at, :] = jnp.where(
                jnp.broadcast_to(x_of, (cap, nx)) == lax.broadcasted_iota(jnp.int32, (cap, nx), 1).astype(jnp.float32), 1.0, 0.0
            )
            lane_mask[rows_at, :] = jnp.where(
                jnp.broadcast_to(layer, (cap, nk)) == lax.broadcasted_iota(jnp.int32, (cap, nk), 1).astype(jnp.float32), 1.0, 0.0
            )

    def pick(number, values):
        gathered[...] = lane_mask[...] * jnp.dot(
            onehot[...], values, precision=HIGHEST, preferred_element_type=jnp.float32
        )
        own_v[number : number + 1, 0:cap] = lanes_to_line(gathered[0:cap, :])
        if number < 7:
            msg_p[number : number + 1, 0:cap] = lanes_to_line(gathered[cap : 2 * cap, :])
            msg_n[number : number + 1, 0:cap] = lanes_to_line(gathered[2 * cap : 3 * cap, :])

    loads[0].wait()
    loads[1].wait()
    tx[PAD + nx - 1 : PAD + nx, :] = jnp.zeros((1, nk), jnp.float32)
    factor_x()

    for one in loads[2:]:
        one.wait()
    lane = lax.broadcasted_iota(jnp.int32, (bl, nk), 1)
    open_y = row < rows - 1

    arrived(T_PNEXT, p_next)

    def make_flux(o):
        tz[pl.ds(o, bl), :] = jnp.where(lane < nk - 1, at(tz, o), 0.0)
        t = jnp.where(open_y, at(ty, o), 0.0)
        ty[pl.ds(o, bl), :] = t
        flux[pl.ds(o, bl), :] = t * (at(p0, o) - at(p_next, o))

    each_block(make_flux)
    remote(flux, f_prev, T_FLUX, next_dev).start()

    arrived(T_TY, ty_y)
    arrived(T_ST, st_y)
    factor_y()
    spread_wide(T_COEF, coef_s, coef_r)

    def start_y(rhs, number, slot, out):
        arrived(number, rhs)
        reduce_y(rhs, slot)
        spread_wide(T_S0 + slot, to_s.at[slot], to_r.at[slot])
        inside_y(rhs, out)

    def middle_y(slot):
        arrived(T_S0 + slot, to_r.at[slot])
        solve_sep(slot)
        spread_wide(T_R0 + slot, re_s.at[slot], re_r.at[slot])

    def end_y(slot, out, number, to_ref):
        arrived(T_R0 + slot, re_r.at[slot])
        complete_y(out, slot)
        to_x(number, out, to_ref)

    start_y(seed_y, T_SEED, 0, late1_y)

    arrived(T_FLUX, f_prev)

    def rhs_u0(o):
        ba[pl.ds(o + pad_x, bl), :] = at(src, o) - (at(flux, o) - at(f_prev, o)) - div_z(at(p0, o), o)

    each_block(rhs_u0)
    solve_x(u0)

    def make_b0(o):
        b0[pl.ds(o, bl), :] = at(src, o) - div_x(u0, o) - div_z(up(u0, o), o)

    each_block(make_b0)
    to_y(T_B0, b0, b0_y)

    arrived(T_COEF, coef_r)
    factor_sep()
    middle_y(0)

    arrived(T_CELL_P, cell_r.at[1])
    arrived(T_CELL_N, cell_r.at[0])
    prepare_picks()
    end_y(0, late1_y, T_LATE1, late1)

    start_y(b0_y, T_B0, 1, p1_y)
    pick(1, p0[...])
    pick(6, ty[...])
    middle_y(1)

    arrived(T_LATE1, inner(late1))

    def rhs_early(ref):
        def body(o):
            ba[pl.ds(o + pad_x, bl), :] = -(div_x(ref, o) + div_z(up(ref, o), o))

        each_block(body)

    rhs_early(late1)
    solve_x(early1)

    def make_rw(o):
        v = up(early1, o)
        rw[pl.ds(o, bl), :] = at(st, o) * v - div_z(v, o)

    each_block(make_rw)
    to_y(T_RW, rw, rw_y)
    end_y(1, p1_y, T_P1, p1)
    pick(4, late1[PAD : PAD + nx, :])

    start_y(rw_y, T_RW, 2, w_y)

    arrived(T_P1, inner(p1))

    def rhs_u1(o):
        v = up(p1, o)
        ba[pl.ds(o + pad_x, bl), :] = at(src, o) - at(b0, o) + at(st, o) * v - div_z(v, o)

    each_block(rhs_u1)
    solve_x(u1)

    def make_b1(o):
        b1[pl.ds(o, bl), :] = at(src, o) - div_x(u1, o) - div_z(up(u1, o), o)

    each_block(make_b1)
    to_y(T_B1, b1, b1_y)

    middle_y(2)
    pick(3, p1[PAD : PAD + nx, :])
    end_y(2, w_y, T_W, w_x)

    start_y(b1_y, T_B1, 3, p2_y)
    middle_y(3)

    arrived(T_W, inner(w_x))

    def make_late0(o):
        late0[pl.ds(o + PAD, bl), :] = up(w_x, o) - up(early1, o)

    each_block(make_late0)
    end_y(3, p2_y, T_P2, p2)
    rhs_early(late0)
    solve_x(early0)

    def make_sums(o):
        sum0[pl.ds(o + PAD, bl), :] = up(late0, o) + up(early0, o)
        both = up(late1, o) + up(early1, o)
        sum1[pl.ds(o + PAD, bl), :] = both
        grad_out[pl.ds(o, bl), :] = up(w_x, o) + up(early0, o) + up(late1, o)

    each_block(make_sums)

    def face_x(o):
        a = (up(sum0, o) - up(sum0, o, 1)) * (up(u0, o) - up(u0, o, 1))
        b = (up(sum1, o) - up(sum1, o, 1)) * (up(u1, o) - up(u1, o, 1))
        ba[pl.ds(o + pad_x, bl), :] = up(tx, o) * (a + b)

    each_block(face_x)

    def step_z(v):
        return v - next_layer(v)

    def cells_xz(o):
        z = step_z(up(early0, o)) * step_z(at(p0, o)) + step_z(up(late0, o)) * step_z(up(u0, o))
        z = z + step_z(up(early1, o)) * step_z(up(p1, o)) + step_z(up(late1, o)) * step_z(up(u1, o))
        z = at(tz, o) * z
        bb[pl.ds(o + pad_x, bl), :] = -0.5 * (big(ba, o) + big(ba, o, -1)) - 0.5 * (z + prev_layer(z))

    each_block(cells_xz)
    pick(7, bb[pad_x : pad_x + nx, :])
    pick(0, early0[PAD : PAD + nx, :])
    pick(2, w_x[PAD : PAD + nx, :])
    arrived(T_P2, inner(p2))
    pick(5, p2[PAD : PAD + nx, :])
    remote(msg_p, msg_r.at[1], T_MSG_P, prev_dev).start()
    remote(msg_n, msg_r.at[0], T_MSG_N, next_dev).start()
    arrived(T_MSG_P, msg_r.at[1])
    arrived(T_MSG_N, msg_r.at[0])

    before = msg_r[0] - own_v[...]
    after = own_v[...] - msg_r[1]

    def pairs(d):
        return d[0:1] * d[1:2] + d[2:3] * d[3:4] + d[4:5] * d[5:6]

    val_s[0] = own_v[7:8, :] - 0.5 * (own_v[6:7, :] * pairs(after) + msg_r[0, 6:7, :] * pairs(before))
    arrived(T_SLOT, slot_r)
    spread_narrow(T_VAL, lambda j: val_s.at[0], val_r.at[ni])
    arrived(T_VAL, val_r)

    base = ((lax.broadcasted_iota(jnp.int32, (nw, nk), 0) * nn + ni) * owned).astype(jnp.float32)
    within = lax.broadcasted_iota(jnp.int32, (nk, nk), 0).astype(jnp.float32)

    def add_terms(i, total):
        s = slot_r[i]
        v = val_r[i]
        rest = s - owned * jnp.floor((s + 0.5) * (1.0 / owned))
        s_all = jnp.broadcast_to(s, (nw, nk))
        a = jnp.where((s_all >= base) & (s_all < base + owned), jnp.broadcast_to(v, (nw, nk)), 0.0)
        b = jnp.where(jnp.broadcast_to(rest, (nk, nk)) == within, 1.0, 0.0)
        return total + lax.dot_general(
            a, b, (((1,), (1,)), ((), ())), precision=HIGHEST, preferred_element_type=jnp.float32
        )

    part_s[:, 0, :] = lax.fori_loop(0, nn, add_terms, jnp.zeros((nw, nk), jnp.float32))
    spread_wide(T_PART, part_s, part_r)
    arrived(T_PART, part_r)
    well_out[...] = jnp.sum(part_r[...], axis=0)

    for number in (T_TY, T_ST, T_SEED, T_B0, T_RW, T_B1, T_LATE1, T_P1, T_W, T_P2):
        sent(number, ty_y.at[pl.ds(0, nn - 1)])
    sent(T_PNEXT, p_next)
    sent(T_FLUX, flux)
    sent(T_CELL_P, cell_s)
    sent(T_CELL_N, cell_s)
    sent(T_MSG_P, msg_p)
    sent(T_MSG_N, msg_n)
    sent(T_SLOT, slot_r.at[pl.ds(0, nn - 1)])
    sent(T_VAL, slot_r.at[pl.ds(0, nn - 1)])
    sent(T_COEF, coef_s.at[pl.ds(0, nw - 1)])
    for slot in range(4):
        sent(T_S0 + slot, to_s.at[slot, pl.ds(0, nw - 1)])
        sent(T_R0 + slot, re_s.at[slot, pl.ds(0, nw - 1)])
    sent(T_PART, part_s.at[pl.ds(0, nw - 1)])


def local(
    source, pressure_start, trans_x, trans_y, trans_z, storage, adjoint_seed,
    comp_cell, comp_well, comp_count, well_slot,
):
    _, nx, nk = source.shape
    nw, nn = lax.axis_size("wide"), lax.axis_size("narrow")
    cap = comp_cell.shape[1]
    owned = well_slot.shape[0] // (nw * nn)
    xc = nx // nn
    pad_w = max(PAD, nw // 2)
    f32 = jnp.float32

    def plain():
        return pltpu.VMEM((nx, nk), f32)

    def padded():
        return pltpu.VMEM((nx + 2 * PAD, nk), f32)

    def wide_pad():
        return pltpu.VMEM((2 * nx, nk), f32)

    def block():
        return pltpu.VMEM((nn, xc, nk), f32)

    def sep_pad():
        return pltpu.VMEM((nw + 2 * pad_w, nk), f32)

    def sep():
        return pltpu.VMEM((nw, nk), f32)

    def many(make, number):
        return [make() for _ in range(number)]

    scratch = (
        [plain(), plain(), padded()] + many(plain, 6)
        + many(block, 6) + many(block, 8)
        + many(padded, 4) + many(plain, 3) + many(padded, 7)
        + [pltpu.VMEM((levels_of(nx), nx, nk), f32)] * 2 + many(plain, 2) + many(wide_pad, 3)
        + [pltpu.VMEM((nw, 4, nk), f32)] * 2 + [pltpu.VMEM((4, nw, 2, nk), f32)] * 4
        + many(sep_pad, 3) + [pltpu.VMEM((levels_of(nw), nw, nk), f32)] * 2 + many(sep, 4)
        + [pltpu.VMEM((1, nk), f32), pltpu.VMEM((2, 1, nk), f32), pltpu.VMEM((8, nk), f32)]
        + [pltpu.VMEM((3 * cap, nx), f32), pltpu.VMEM((3 * cap, nk), f32), pltpu.VMEM((3 * cap, nk), f32)]
        + [pltpu.VMEM((8, nk), f32)] * 3 + [pltpu.VMEM((2, 8, nk), f32)]
        + [pltpu.VMEM((1, 1, nk), f32), pltpu.VMEM((nn, 1, nk), f32)] * 2
        + [pltpu.VMEM((nw, 1, nk), f32)] * 2
        + [pltpu.SemaphoreType.DMA((T_COUNT,)), pltpu.SemaphoreType.DMA((T_COUNT,)), pltpu.SemaphoreType.DMA((L_COUNT,))]
    )
    hbm = pl.BlockSpec(memory_space=pl.ANY)
    vmem = pl.BlockSpec(memory_space=pltpu.VMEM)
    smem = pl.BlockSpec(memory_space=pltpu.SMEM)
    grad, sums = pl.pallas_call(
        functools.partial(kernel, nw, nn, nx, nk, cap, owned),
        out_shape=(jax.ShapeDtypeStruct((nx, nk), f32), jax.ShapeDtypeStruct((1, nk), f32)),
        in_specs=[hbm] * 7 + [vmem, vmem, smem, vmem],
        out_specs=(vmem, vmem),
        scratch_shapes=scratch,
        compiler_params=pltpu.CompilerParams(
            collective_id=0, has_side_effects=True, vmem_limit_bytes=48 * 1024 * 1024
        ),
    )(
        source[0], pressure_start[0], trans_x[0], trans_y[0], trans_z[0], storage[0], adjoint_seed[0],
        comp_cell, comp_well, comp_count.reshape(1, 1), well_slot.reshape(-1, nk),
    )
    return grad[None], sums[0, :owned]


def solution(mesh):
    cells = P(("wide", "narrow"), None, None)
    placed = (cells,) * 7 + (P(("wide", "narrow"), None), P(("wide", "narrow"), None), P(("wide", "narrow")), P())
    return jax.shard_map(
        local, mesh=mesh, in_specs=placed, out_specs=(cells, P(("wide", "narrow"))), check_vma=False
    )
```

time: 1050 us -> 172 us (0.16)
  waiting for transfers between devices: 620 us -> 0 us
  blocking collectives: 207 us -> 0 us
  Pallas kernels: 0 us -> 161 us
  starting transfers between devices: 105 us -> 0 us
  local copies, waits for them, and re-layouts: 69.3 us -> 9.4 us
  other arithmetic: 30.1 us -> 0 us
  between operations: 17.6 us -> 1.31 us
    unnamed x2 -> x0, waiting for transfers between devices: 431 us -> none
    all_to_all x6 -> x0, blocking collectives: 207 us -> none  [the longest x1 80.8 us: to_lines_y(): lax.all_to_all(partial_move, 'wide', split_axis=2, concat_axis=1, tiled=T...]
    all_to_all x16 -> x0, waiting for transfers between devices: 189 us -> none  [the longest x5 85.4 us: to_lines_y(): lax.all_to_all(partial_move, 'wide', split_axis=2, concat_axis=1, tiled=T...]
    pallas_call x0 -> x1, Pallas kernels: none -> 161 us  [local(): pl.pallas_call(functools.partial(kernel, nw, nn, nx, nk, cap, owned), out...]
    all_to_all x16 -> x0, starting transfers between devices: 105 us -> none  [the longest x5 35.9 us: to_lines_y(): lax.all_to_all(partial_move, 'wide', split_axis=2, concat_axis=1, tiled=T...]
    unnamed x315 -> x21, local copies, waits for them, and re-layouts: 35.8 us -> 8.89 us
    slice x145 -> x0, local copies, waits for them, and re-layouts: 16.4 us -> none  [the longest x86 9.32 us: shifted(): kept = lax.slice_in_dim(values, 0, extent - offset, axis=axis_dim)]
    sub x62 -> x0, other arithmetic: 15.8 us -> none  [the longest x40 10 us: solve_lines(): right_side - left_gain * shifted(right_side, stride, axis_dim)]
  transfers between devices with their start and end apart: 17 -> 0, of which waited for: 16 -> 0; matrix products, arithmetic and copies ran while one was open for 3% -> 0% of each run, Pallas kernels for 0% -> 0%
where the time goes in v1:
time: 172 us
  Pallas kernels  161 us (94%)
  local copies, waits for them, and re-layouts  9.4 us (5%)
    pallas_call x1, Pallas kernels, local(): pl.pallas_call(functools.partial(kernel, nw, nn, nx, nk, cap, owned), out...  161 us
    unnamed x21, local copies, waits for them, and re-layouts  8.89 us

profile of v1, /device:TPU:1, one launch (start us, length us, event | category | flops | bytes accessed | tf_op | source)
XLA Modules:
  0.0 171.9 jit_solution(6766340193457566137)
XLA Ops:
  1.3 0.0 copy-start.8
  1.3 0.0 copy-start.9
  1.3 0.6 copy-done.8
  1.9 0.0 copy-done.9
  2.0 0.0 copy-start
  2.0 0.9 copy-done
  2.9 0.0 copy-start.1
  2.9 0.9 copy-done.1
  3.9 0.0 copy-start.2
  3.9 0.9 copy-done.2
  4.8 0.0 copy-start.3
  4.8 0.9 copy-done.3
  5.8 0.0 copy-start.4
  5.8 0.9 copy-done.4
  6.7 0.0 copy-start.5
  6.7 0.9 copy-done.5
  7.7 0.0 copy-start.6
  7.7 0.9 copy-done.6
  8.6 0.0 copy-start.7
  8.6 0.9 copy-done.7
  9.5 161.2 %shard_map.122 = (f32[512,128]{1,0:T(8,128)S(1)}, f32[1,128]{1,0:T(1,128)S(1)}) custom-call(f32[512,128]{1,0:T(8,128)S(1)} %bitcast.14, f32[512,128]{1,0:T(8,128)S(1)} %bitcast.15, f32[512,128]{1,0:T(8,128)S(1)} %bitcast.16, f32[512,128]{1,0:T(8,128)S(1)} %bitcast.17, f32[512,128]{1,0:T(8,128)S(1)} %bitcast.18, f32[512,128]{1,0:T(8,128)S(1)} %bitcast.19, ...), custom_call_target="tpu_custom_call" | custom-call | tf_op jit(solution)/shard_map/pallas_call | solution.py:650
  170.7 0.5 slice_bitcast_fusion
  171.2 0.7 copy.15
Async XLA Ops:
  1.3 0.7 copy-start.8
  1.3 0.7 copy-start.9
  2.0 0.9 copy-start
  2.9 0.9 copy-start.1
  3.9 0.9 copy-start.2
  4.8 0.9 copy-start.3
  5.8 0.9 copy-start.4
  6.7 0.9 copy-start.5
  7.7 0.9 copy-start.6
  8.6 0.9 copy-start.7

commit v2 on v1

--- a/solution.py
+++ b/solution.py
@@ -12,7 +12,7 @@
 PAD = 8
 
 (
-    T_TY, T_ST, T_SEED, T_B0, T_RW, T_B1, T_LATE1, T_P1, T_W, T_P2,
+    T_TY, T_ST, T_SEED, T_B0, T_RW, T_B1, T_LATE1, T_P1, T_W, T_TIN,
     T_PNEXT, T_FLUX, T_CELL_P, T_CELL_N, T_SLOT, T_VAL, T_MSG_P, T_MSG_N,
     T_COEF, T_S0, T_S1, T_S2, T_S3, T_R0, T_R1, T_R2, T_R3, T_PART, T_COUNT,
 ) = range(29)
@@ -30,12 +30,13 @@
     src, p0, tx, ty, tz, st, p_next, flux, f_prev,
     ty_y, st_y, seed_y, b0_y, rw_y, b1_y,
     inv_y, m_y, ga_y, gb_y, late1_y, p1_y, w_y, p2_y,
-    late1, p1, w_x, p2, b0, b1, rw, u0, u1, early1, early0, late0, sum0, sum1,
+    late1, p1, w_x, b0, b1, rw, u0, u1, early1, early0, late0, sum0, sum1,
     gain_l, gain_r, inv_x, mid_x, ba, bb, bc,
     coef_s, coef_r, to_s, to_r, re_s, re_r,
     ia, ib, ic, pk_l, pk_r, pk_inv, tau, kap, f0s,
     cell_s, cell_r, pick_rows, onehot, lane_mask, gathered, own_v, msg_p, msg_n, msg_r,
     slot_s, slot_r, val_s, val_r, part_s, part_r,
+    tin_s, tin_r, c_y, hot_y, mask_y, picked_y, slot_line, owner_hot, place_hot,
     send_sem, recv_sem, load_sem,
 ):
     wi, ni = lax.axis_index("wide"), lax.axis_index("narrow")
@@ -119,7 +120,7 @@
         return ref.at[pl.ds(PAD, nx)]
 
     zeros_pad = jnp.zeros((PAD, nk), jnp.float32)
-    for ref in (tx, late1, p1, w_x, p2, u0, u1, early1, early0, late0, sum0, sum1):
+    for ref in (tx, late1, p1, w_x, u0, u1, early1, early0, late0, sum0, sum1):
         ref[0:PAD, :] = zeros_pad
         ref[PAD + nx : 2 * PAD + nx, :] = zeros_pad
     zeros_x = jnp.zeros((pad_x, nk), jnp.float32)
@@ -163,12 +164,13 @@
     live = lax.broadcasted_iota(jnp.int32, (1, cap), 1) < count[0, 0]
     slot_s[...] = jnp.full_like(slot_s, -1.0)
     slot_s[0, 0:1, 0:cap] = jnp.where(live, lanes_to_line(table), -1.0)
+    slot_s[0, 1:2, 0:cap] = cell_s[0:1, 0:cap]
 
     pl.semaphore_wait(barrier, nn - 1 + nw - 1 + 2)
 
-    remote(pressure, p_next, T_PNEXT, prev_dev).start()
     to_y(T_TY, trans_y, ty_y)
     to_y(T_ST, storage, st_y)
+    remote(pressure, p_next, T_PNEXT, prev_dev).start()
     to_y(T_SEED, seed, seed_y)
     remote(cell_s, cell_r.at[1], T_CELL_P, prev_dev).start()
     remote(cell_s, cell_r.at[0], T_CELL_N, next_dev).start()
@@ -334,6 +336,7 @@
         tau_v = t_in / (1.0 + t_in * corner)
         tau[...] = tau_v
         kap[...] = kappa
+        tin_s[:, 0, :] = t_in
         put(ia, tau_v)
         put(ib, tau_v * kappa)
         middle = dee + mid(ia, 1) + kappa * kappa * tau_v
@@ -389,15 +392,93 @@
             msg_p[number : number + 1, 0:cap] = lanes_to_line(gathered[cap : 2 * cap, :])
             msg_n[number : number + 1, 0:cap] = lanes_to_line(gathered[2 * cap : 3 * cap, :])
 
+    terms = nn * cap
+
+    def prepare_group():
+        arrived(T_SLOT, slot_r)
+        for j in range(nn):
+            slot_line[0:1, j * cap : (j + 1) * cap] = slot_r[j, 0:1, 0:cap]
+
+        def body(j, c):
+            col = column(slot_r[j, 1:2, :])
+            x_of = jnp.floor(col * (1.0 / nk))
+            layer = col - x_of * nk
+            x_of = x_of - (ni * xc).astype(jnp.float32)
+            hot_y[j] = jnp.where(
+                jnp.broadcast_to(x_of, (cap, xc)) == lax.broadcasted_iota(jnp.int32, (cap, xc), 1).astype(jnp.float32), 1.0, 0.0
+            )
+            mask_y[j] = jnp.where(
+                jnp.broadcast_to(layer, (cap, nk)) == lax.broadcasted_iota(jnp.int32, (cap, nk), 1).astype(jnp.float32), 1.0, 0.0
+            )
+            return c
+
+        lax.fori_loop(0, nn, body, 0)
+
+    def prepare_owners():
+        s_line = slot_line[...]
+        base = ((lax.broadcasted_iota(jnp.int32, (nw, terms), 0) * nn + ni) * owned).astype(jnp.float32)
+        s_all = jnp.broadcast_to(s_line, (nw, terms))
+        owner_hot[...] = jnp.where((s_all >= base) & (s_all < base + owned), 1.0, 0.0)
+        rest = s_line - owned * jnp.floor((s_line + 0.5) * (1.0 / owned))
+        place_hot[...] = jnp.where(
+            jnp.broadcast_to(rest, (nk, terms)) == lax.broadcasted_iota(jnp.int32, (nk, terms), 0).astype(jnp.float32), 1.0, 0.0
+        )
+
+    def cells_y():
+        t_in = tin_r[:, 0, :]
+        there = t_in > 0.0
+        e0 = jnp.where(there, re_r[0, :, 0, :] * re_r[3, :, 0, :] / jnp.where(there, t_in, 1.0), 0.0)
+
+        def body(j, before):
+            e = ty_y[j] * (late1_y[j] - late1_y[j + 1]) * (p2_y[j] - p2_y[j + 1])
+            c_y[j] = -0.5 * (e + before)
+            return e
+
+        before = lax.fori_loop(0, last, body, e0)
+
+        def out_flux(rhs, v):
+            return rhs[last] - st_y[last] * v[last] - ty_y[last - 1] * (v[last] - v[last - 1])
+
+        e = jnp.where(wi == nw - 1, 0.0, out_flux(seed_y, late1_y) * out_flux(b1_y, p2_y) / ty_y[last])
+        c_y[last] = -0.5 * (e + before)
+
+    def pick_y():
+        for j in range(nn):
+            picked_y[j * cap : (j + 1) * cap, :] = mask_y[j] * jnp.dot(
+                hot_y[j], c_y[j], precision=HIGHEST, preferred_element_type=jnp.float32
+            )
+        return lanes_to_line(picked_y[...])
+
+    def start_y(rhs, number, slot, out):
+        arrived(number, rhs)
+        reduce_y(rhs, slot)
+        spread_wide(T_S0 + slot, to_s.at[slot], to_r.at[slot])
+        inside_y(rhs, out)
+
+    def middle_y(slot):
+        arrived(T_S0 + slot, to_r.at[slot])
+        solve_sep(slot)
+        spread_wide(T_R0 + slot, re_s.at[slot], re_r.at[slot])
+
+    def end_y(slot, out, number=None, to_ref=None):
+        arrived(T_R0 + slot, re_r.at[slot])
+        complete_y(out, slot)
+        if number is not None:
+            to_x(number, out, to_ref)
+
     loads[0].wait()
     loads[1].wait()
     tx[PAD + nx - 1 : PAD + nx, :] = jnp.zeros((1, nk), jnp.float32)
     factor_x()
-
     for one in loads[2:]:
         one.wait()
     lane = lax.broadcasted_iota(jnp.int32, (bl, nk), 1)
     open_y = row < rows - 1
+
+    arrived(T_TY, ty_y)
+    arrived(T_ST, st_y)
+    factor_y()
+    spread_wide(T_COEF, coef_s, coef_r)
 
     arrived(T_PNEXT, p_next)
 
@@ -410,28 +491,11 @@
     each_block(make_flux)
     remote(flux, f_prev, T_FLUX, next_dev).start()
 
-    arrived(T_TY, ty_y)
-    arrived(T_ST, st_y)
-    factor_y()
-    spread_wide(T_COEF, coef_s, coef_r)
-
-    def start_y(rhs, number, slot, out):
-        arrived(number, rhs)
-        reduce_y(rhs, slot)
-        spread_wide(T_S0 + slot, to_s.at[slot], to_r.at[slot])
-        inside_y(rhs, out)
-
-    def middle_y(slot):
-        arrived(T_S0 + slot, to_r.at[slot])
-        solve_sep(slot)
-        spread_wide(T_R0 + slot, re_s.at[slot], re_r.at[slot])
-
-    def end_y(slot, out, number, to_ref):
-        arrived(T_R0 + slot, re_r.at[slot])
-        complete_y(out, slot)
-        to_x(number, out, to_ref)
-
     start_y(seed_y, T_SEED, 0, late1_y)
+
+    arrived(T_CELL_P, cell_r.at[1])
+    arrived(T_CELL_N, cell_r.at[0])
+    prepare_picks()
 
     arrived(T_FLUX, f_prev)
 
@@ -450,14 +514,11 @@
     arrived(T_COEF, coef_r)
     factor_sep()
     middle_y(0)
-
-    arrived(T_CELL_P, cell_r.at[1])
-    arrived(T_CELL_N, cell_r.at[0])
-    prepare_picks()
-    end_y(0, late1_y, T_LATE1, late1)
+    spread_wide(T_TIN, tin_s, tin_r)
 
     start_y(b0_y, T_B0, 1, p1_y)
     pick(1, p0[...])
+    end_y(0, late1_y, T_LATE1, late1)
     pick(6, ty[...])
     middle_y(1)
 
@@ -479,9 +540,10 @@
     each_block(make_rw)
     to_y(T_RW, rw, rw_y)
     end_y(1, p1_y, T_P1, p1)
-    pick(4, late1[PAD : PAD + nx, :])
 
     start_y(rw_y, T_RW, 2, w_y)
+    prepare_group()
+    prepare_owners()
 
     arrived(T_P1, inner(p1))
 
@@ -500,10 +562,8 @@
 
     middle_y(2)
     pick(3, p1[PAD : PAD + nx, :])
+    start_y(b1_y, T_B1, 3, p2_y)
     end_y(2, w_y, T_W, w_x)
-
-    start_y(b1_y, T_B1, 3, p2_y)
-    middle_y(3)
 
     arrived(T_W, inner(w_x))
 
@@ -511,9 +571,9 @@
         late0[pl.ds(o + PAD, bl), :] = up(w_x, o) - up(early1, o)
 
     each_block(make_late0)
-    end_y(3, p2_y, T_P2, p2)
     rhs_early(late0)
     solve_x(early0)
+    middle_y(3)
 
     def make_sums(o):
         sum0[pl.ds(o + PAD, bl), :] = up(late0, o) + up(early0, o)
@@ -543,44 +603,37 @@
     pick(7, bb[pad_x : pad_x + nx, :])
     pick(0, early0[PAD : PAD + nx, :])
     pick(2, w_x[PAD : PAD + nx, :])
-    arrived(T_P2, inner(p2))
-    pick(5, p2[PAD : PAD + nx, :])
     remote(msg_p, msg_r.at[1], T_MSG_P, prev_dev).start()
     remote(msg_n, msg_r.at[0], T_MSG_N, next_dev).start()
+    arrived(T_TIN, tin_r)
     arrived(T_MSG_P, msg_r.at[1])
     arrived(T_MSG_N, msg_r.at[0])
-
     before = msg_r[0] - own_v[...]
     after = own_v[...] - msg_r[1]
 
     def pairs(d):
-        return d[0:1] * d[1:2] + d[2:3] * d[3:4] + d[4:5] * d[5:6]
-
-    val_s[0] = own_v[7:8, :] - 0.5 * (own_v[6:7, :] * pairs(after) + msg_r[0, 6:7, :] * pairs(before))
-    arrived(T_SLOT, slot_r)
+        return d[0:1] * d[1:2] + d[2:3] * d[3:4]
+
+    own_line = own_v[7:8, :] - 0.5 * (own_v[6:7, :] * pairs(after) + msg_r[0, 6:7, :] * pairs(before))
+    here = lax.broadcasted_iota(jnp.int32, (1, terms), 1) // cap == ni
+    val_s[0] = jnp.where(here, jnp.concatenate([own_line[:, 0:cap]] * nn, axis=1), 0.0)
+
+    end_y(3, p2_y)
+    cells_y()
+    val_s[0] = val_s[0] + pick_y()
     spread_narrow(T_VAL, lambda j: val_s.at[0], val_r.at[ni])
     arrived(T_VAL, val_r)
 
-    base = ((lax.broadcasted_iota(jnp.int32, (nw, nk), 0) * nn + ni) * owned).astype(jnp.float32)
-    within = lax.broadcasted_iota(jnp.int32, (nk, nk), 0).astype(jnp.float32)
-
-    def add_terms(i, total):
-        s = slot_r[i]
-        v = val_r[i]
-        rest = s - owned * jnp.floor((s + 0.5) * (1.0 / owned))
-        s_all = jnp.broadcast_to(s, (nw, nk))
-        a = jnp.where((s_all >= base) & (s_all < base + owned), jnp.broadcast_to(v, (nw, nk)), 0.0)
-        b = jnp.where(jnp.broadcast_to(rest, (nk, nk)) == within, 1.0, 0.0)
-        return total + lax.dot_general(
-            a, b, (((1,), (1,)), ((), ())), precision=HIGHEST, preferred_element_type=jnp.float32
-        )
-
-    part_s[:, 0, :] = lax.fori_loop(0, nn, add_terms, jnp.zeros((nw, nk), jnp.float32))
+    totals = jnp.sum(val_r[...], axis=0)
+    part_s[:, 0, :] = lax.dot_general(
+        owner_hot[...] * jnp.broadcast_to(totals, (nw, terms)), place_hot[...],
+        (((1,), (1,)), ((), ())), precision=HIGHEST, preferred_element_type=jnp.float32,
+    )
     spread_wide(T_PART, part_s, part_r)
     arrived(T_PART, part_r)
     well_out[...] = jnp.sum(part_r[...], axis=0)
 
-    for number in (T_TY, T_ST, T_SEED, T_B0, T_RW, T_B1, T_LATE1, T_P1, T_W, T_P2):
+    for number in (T_TY, T_ST, T_SEED, T_B0, T_RW, T_B1, T_LATE1, T_P1, T_W):
         sent(number, ty_y.at[pl.ds(0, nn - 1)])
     sent(T_PNEXT, p_next)
     sent(T_FLUX, flux)
@@ -589,7 +642,8 @@
     sent(T_MSG_P, msg_p)
     sent(T_MSG_N, msg_n)
     sent(T_SLOT, slot_r.at[pl.ds(0, nn - 1)])
-    sent(T_VAL, slot_r.at[pl.ds(0, nn - 1)])
+    sent(T_VAL, val_r.at[pl.ds(0, nn - 1)])
+    sent(T_TIN, tin_s.at[pl.ds(0, nw - 1)])
     sent(T_COEF, coef_s.at[pl.ds(0, nw - 1)])
     for slot in range(4):
         sent(T_S0 + slot, to_s.at[slot, pl.ds(0, nw - 1)])
@@ -633,15 +687,18 @@
     scratch = (
         [plain(), plain(), padded()] + many(plain, 6)
         + many(block, 6) + many(block, 8)
-        + many(padded, 4) + many(plain, 3) + many(padded, 7)
+        + many(padded, 3) + many(plain, 3) + many(padded, 7)
         + [pltpu.VMEM((levels_of(nx), nx, nk), f32)] * 2 + many(plain, 2) + many(wide_pad, 3)
         + [pltpu.VMEM((nw, 4, nk), f32)] * 2 + [pltpu.VMEM((4, nw, 2, nk), f32)] * 4
         + many(sep_pad, 3) + [pltpu.VMEM((levels_of(nw), nw, nk), f32)] * 2 + many(sep, 4)
         + [pltpu.VMEM((1, nk), f32), pltpu.VMEM((2, 1, nk), f32), pltpu.VMEM((8, nk), f32)]
         + [pltpu.VMEM((3 * cap, nx), f32), pltpu.VMEM((3 * cap, nk), f32), pltpu.VMEM((3 * cap, nk), f32)]
         + [pltpu.VMEM((8, nk), f32)] * 3 + [pltpu.VMEM((2, 8, nk), f32)]
-        + [pltpu.VMEM((1, 1, nk), f32), pltpu.VMEM((nn, 1, nk), f32)] * 2
-        + [pltpu.VMEM((nw, 1, nk), f32)] * 2
+        + [pltpu.VMEM((1, 2, nk), f32), pltpu.VMEM((nn, 2, nk), f32)]
+        + [pltpu.VMEM((1, 1, nn * cap), f32), pltpu.VMEM((nn, 1, nn * cap), f32)]
+        + [pltpu.VMEM((nw, 1, nk), f32)] * 4
+        + [block(), pltpu.VMEM((nn, cap, xc), f32), pltpu.VMEM((nn, cap, nk), f32), pltpu.VMEM((nn * cap, nk), f32)]
+        + [pltpu.VMEM((1, nn * cap), f32), pltpu.VMEM((nw, nn * cap), f32), pltpu.VMEM((nk, nn * cap), f32)]
         + [pltpu.SemaphoreType.DMA((T_COUNT,)), pltpu.SemaphoreType.DMA((T_COUNT,)), pltpu.SemaphoreType.DMA((L_COUNT,))]
     )
     hbm = pl.BlockSpec(memory_space=pl.ANY)
@@ -654,7 +711,7 @@
         out_specs=(vmem, vmem),
         scratch_shapes=scratch,
         compiler_params=pltpu.CompilerParams(
-            collective_id=0, has_side_effects=True, vmem_limit_bytes=48 * 1024 * 1024
+            collective_id=0, has_side_effects=True, vmem_limit_bytes=62 * 1024 * 1024
         ),
     )(
         source[0], pressure_start[0], trans_x[0], trans_y[0], trans_z[0], storage[0], adjoint_seed[0],

time: 172 us -> 149 us (0.87)
  Pallas kernels: 161 us -> 145 us
  local copies, waits for them, and re-layouts: 9.4 us -> 2.74 us
    pallas_call x1, Pallas kernels: 161 us -> 145 us  [local(): pl.pallas_call(functools.partial(kernel, nw, nn, nx, nk, cap, owned), out...]
    unnamed x21 -> x3, local copies, waits for them, and re-layouts: 8.89 us -> 2.23 us
where the time goes in v2:
time: 149 us
  Pallas kernels  145 us (97%)
  local copies, waits for them, and re-layouts  2.74 us (2%)
    pallas_call x1, Pallas kernels, local(): pl.pallas_call(functools.partial(kernel, nw, nn, nx, nk, cap, owned), out...  145 us

profile of v2, /device:TPU:1, one launch (start us, length us, event | category | flops | bytes accessed | tf_op | source)
XLA Modules:
  0.0 149.2 jit_solution(18204097955489420920)
XLA Ops:
  1.3 145.2 %shard_map.122 = (f32[512,128]{1,0:T(8,128)}, f32[1,128]{1,0:T(1,128)}) custom-call(f32[512,128]{1,0:T(8,128)} %bitcast.14, f32[512,128]{1,0:T(8,128)} %bitcast.15, f32[512,128]{1,0:T(8,128)} %bitcast.16, f32[512,128]{1,0:T(8,128)} %bitcast.17, f32[512,128]{1,0:T(8,128)} %bitcast.18, f32[512,128]{1,0:T(8,128)} %bitcast.19, f32[512,128]{1,0:T(8,128)} %bitcast.20, ...), custom_call_target="tpu_custom_call" | custom-call | tf_op jit(solution)/shard_map/pallas_call | solution.py:707
  146.5 0.0 copy-start
  146.5 0.6 copy-done
  147.1 0.5 slice_bitcast_fusion
  147.6 1.7 %copy.15 = f32[1,512,128]{2,1,0:T(8,128)} copy(f32[1,512,128]{2,1,0:T(8,128)} %bitcast.13) | data formatting | bytes 524288
Async XLA Ops:
  146.5 0.6 copy-start

commit v3 on v2

--- a/solution.py
+++ b/solution.py
@@ -27,18 +27,20 @@
     nw, nn, nx, nk, cap, owned,
     source, pressure, trans_x, trans_y, trans_z, storage, seed, cell, well, count, slots,
     grad_out, well_out,
-    src, p0, tx, ty, tz, st, p_next, flux, f_prev,
+    src, tx, tz, st, p_next, flux, f_prev,
     ty_y, st_y, seed_y, b0_y, rw_y, b1_y,
     inv_y, m_y, ga_y, gb_y, late1_y, p1_y, w_y, p2_y,
-    late1, p1, w_x, b0, b1, rw, u0, u1, early1, early0, late0, sum0, sum1,
+    late1, b0, b1, rw, u0, u1, early1, late0, sum0, sum1,
     gain_l, gain_r, inv_x, mid_x, ba, bb, bc,
     coef_s, coef_r, to_s, to_r, re_s, re_r,
     ia, ib, ic, pk_l, pk_r, pk_inv, tau, kap, f0s,
     cell_s, cell_r, pick_rows, onehot, lane_mask, gathered, own_v, msg_p, msg_n, msg_r,
     slot_s, slot_r, val_s, val_r, part_s, part_r,
     tin_s, tin_r, c_y, hot_y, mask_y, picked_y, slot_line, owner_hot, place_hot,
-    send_sem, recv_sem, load_sem,
+    fields, send_sem, recv_sem, load_sem,
 ):
+    p0, ty = fields.at[0, pl.ds(PAD, nx)], fields.at[2, pl.ds(PAD, nx)]
+    p1, early0, w_x = fields.at[1], fields.at[3], fields.at[4]
     wi, ni = lax.axis_index("wide"), lax.axis_index("narrow")
     rows = nw * nn
     row = wi * nn + ni
@@ -48,7 +50,7 @@
     xc = nx // nn
     lev, pad_x = levels_of(nx), nx // 2
     lev_w, pad_w = levels_of(nw), max(PAD, nw // 2)
-    bl = min(64, nx)
+    bl = min(512, nx)
     blocks = nx // bl
 
     barrier = pltpu.get_barrier_semaphore()
@@ -293,7 +295,7 @@
             v = rhs[j]
             return a + gb_y[j] * v, f + ga_y[j] * v
 
-        a, f = lax.fori_loop(0, last, body, (rhs[last], jnp.zeros((xc, nk), jnp.float32)))
+        a, f = lax.fori_loop(0, last, body, (rhs[last], jnp.zeros((xc, nk), jnp.float32)), unroll=True)
         to_s[slot, :, 0, :] = a
         to_s[slot, :, 1, :] = f
 
@@ -320,7 +322,7 @@
             out[j] = out[j] + ga_y[j] * phi + gb_y[j] * sep
             return c
 
-        lax.fori_loop(0, last, body, 0)
+        lax.fori_loop(0, last, body, 0, unroll=True)
         out[last] = sep
 
     def mid(ref, shift=0):
@@ -383,14 +385,18 @@
                 jnp.broadcast_to(layer, (cap, nk)) == lax.broadcasted_iota(jnp.int32, (cap, nk), 1).astype(jnp.float32), 1.0, 0.0
             )
 
-    def pick(number, values):
-        gathered[...] = lane_mask[...] * jnp.dot(
-            onehot[...], values, precision=HIGHEST, preferred_element_type=jnp.float32
-        )
-        own_v[number : number + 1, 0:cap] = lanes_to_line(gathered[0:cap, :])
-        if number < 7:
-            msg_p[number : number + 1, 0:cap] = lanes_to_line(gathered[cap : 2 * cap, :])
-            msg_n[number : number + 1, 0:cap] = lanes_to_line(gathered[2 * cap : 3 * cap, :])
+    def pick_three(first):
+        def body(i, c):
+            number = first + i
+            gathered[...] = lane_mask[...] * jnp.dot(
+                onehot[...], fields[number, pl.ds(PAD, nx), :], precision=HIGHEST, preferred_element_type=jnp.float32
+            )
+            own_v[pl.ds(number, 1), 0:cap] = lanes_to_line(gathered[0:cap, :])
+            msg_p[pl.ds(number, 1), 0:cap] = lanes_to_line(gathered[cap : 2 * cap, :])
+            msg_n[pl.ds(number, 1), 0:cap] = lanes_to_line(gathered[2 * cap : 3 * cap, :])
+            return c
+
+        lax.fori_loop(0, 3, body, 0)
 
     terms = nn * cap
 
@@ -514,12 +520,9 @@
     arrived(T_COEF, coef_r)
     factor_sep()
     middle_y(0)
-    spread_wide(T_TIN, tin_s, tin_r)
 
     start_y(b0_y, T_B0, 1, p1_y)
-    pick(1, p0[...])
     end_y(0, late1_y, T_LATE1, late1)
-    pick(6, ty[...])
     middle_y(1)
 
     arrived(T_LATE1, inner(late1))
@@ -540,6 +543,7 @@
     each_block(make_rw)
     to_y(T_RW, rw, rw_y)
     end_y(1, p1_y, T_P1, p1)
+    spread_wide(T_TIN, tin_s, tin_r)
 
     start_y(rw_y, T_RW, 2, w_y)
     prepare_group()
@@ -561,7 +565,7 @@
     to_y(T_B1, b1, b1_y)
 
     middle_y(2)
-    pick(3, p1[PAD : PAD + nx, :])
+    pick_three(0)
     start_y(b1_y, T_B1, 3, p2_y)
     end_y(2, w_y, T_W, w_x)
 
@@ -597,30 +601,29 @@
         z = step_z(up(early0, o)) * step_z(at(p0, o)) + step_z(up(late0, o)) * step_z(up(u0, o))
         z = z + step_z(up(early1, o)) * step_z(up(p1, o)) + step_z(up(late1, o)) * step_z(up(u1, o))
         z = at(tz, o) * z
-        bb[pl.ds(o + pad_x, bl), :] = -0.5 * (big(ba, o) + big(ba, o, -1)) - 0.5 * (z + prev_layer(z))
+        fields[5, pl.ds(o + PAD, bl), :] = -0.5 * (big(ba, o) + big(ba, o, -1)) - 0.5 * (z + prev_layer(z))
 
     each_block(cells_xz)
-    pick(7, bb[pad_x : pad_x + nx, :])
-    pick(0, early0[PAD : PAD + nx, :])
-    pick(2, w_x[PAD : PAD + nx, :])
+    pick_three(3)
     remote(msg_p, msg_r.at[1], T_MSG_P, prev_dev).start()
     remote(msg_n, msg_r.at[0], T_MSG_N, next_dev).start()
     arrived(T_TIN, tin_r)
+
+    end_y(3, p2_y)
+    cells_y()
+    from_block = pick_y()
+
     arrived(T_MSG_P, msg_r.at[1])
     arrived(T_MSG_N, msg_r.at[0])
     before = msg_r[0] - own_v[...]
     after = own_v[...] - msg_r[1]
 
     def pairs(d):
-        return d[0:1] * d[1:2] + d[2:3] * d[3:4]
-
-    own_line = own_v[7:8, :] - 0.5 * (own_v[6:7, :] * pairs(after) + msg_r[0, 6:7, :] * pairs(before))
+        return d[3:4] * d[0:1] + d[4:5] * d[1:2]
+
+    own_line = own_v[5:6, :] - 0.5 * (own_v[2:3, :] * pairs(after) + msg_r[0, 2:3, :] * pairs(before))
     here = lax.broadcasted_iota(jnp.int32, (1, terms), 1) // cap == ni
-    val_s[0] = jnp.where(here, jnp.concatenate([own_line[:, 0:cap]] * nn, axis=1), 0.0)
-
-    end_y(3, p2_y)
-    cells_y()
-    val_s[0] = val_s[0] + pick_y()
+    val_s[0] = from_block + jnp.where(here, jnp.concatenate([own_line[:, 0:cap]] * nn, axis=1), 0.0)
     spread_narrow(T_VAL, lambda j: val_s.at[0], val_r.at[ni])
     arrived(T_VAL, val_r)
 
@@ -685,9 +688,9 @@
         return [make() for _ in range(number)]
 
     scratch = (
-        [plain(), plain(), padded()] + many(plain, 6)
+        [plain(), padded()] + many(plain, 5)
         + many(block, 6) + many(block, 8)
-        + many(padded, 3) + many(plain, 3) + many(padded, 7)
+        + many(padded, 1) + many(plain, 3) + many(padded, 6)
         + [pltpu.VMEM((levels_of(nx), nx, nk), f32)] * 2 + many(plain, 2) + many(wide_pad, 3)
         + [pltpu.VMEM((nw, 4, nk), f32)] * 2 + [pltpu.VMEM((4, nw, 2, nk), f32)] * 4
         + many(sep_pad, 3) + [pltpu.VMEM((levels_of(nw), nw, nk), f32)] * 2 + many(sep, 4)
@@ -699,6 +702,7 @@
         + [pltpu.VMEM((nw, 1, nk), f32)] * 4
         + [block(), pltpu.VMEM((nn, cap, xc), f32), pltpu.VMEM((nn, cap, nk), f32), pltpu.VMEM((nn * cap, nk), f32)]
         + [pltpu.VMEM((1, nn * cap), f32), pltpu.VMEM((nw, nn * cap), f32), pltpu.VMEM((nk, nn * cap), f32)]
+        + [pltpu.VMEM((6, nx + 2 * PAD, nk), f32)]
         + [pltpu.SemaphoreType.DMA((T_COUNT,)), pltpu.SemaphoreType.DMA((T_COUNT,)), pltpu.SemaphoreType.DMA((L_COUNT,))]
     )
     hbm = pl.BlockSpec(memory_space=pl.ANY)

time: 149 us -> 143 us (0.960)
  Pallas kernels: 145 us -> 138 us
    pallas_call x1, Pallas kernels: 145 us -> 138 us  [local(): pl.pallas_call(functools.partial(kernel, nw, nn, nx, nk, cap, owned), out...]
where the time goes in v3:
time: 143 us; the launch traced here: 142 us
  Pallas kernels  138 us (97%)
  local copies, waits for them, and re-layouts  2.74 us (2%)
    pallas_call x1, Pallas kernels, local(): pl.pallas_call(functools.partial(kernel, nw, nn, nx, nk, cap, owned), out...  138 us

profile of v3, /device:TPU:1, one launch (start us, length us, event | category | flops | bytes accessed | tf_op | source)
XLA Modules:
  0.0 142.5 jit_solution(1430079040675321915)
XLA Ops:
  1.3 138.5 %shard_map.122 = (f32[512,128]{1,0:T(8,128)}, f32[1,128]{1,0:T(1,128)}) custom-call(f32[512,128]{1,0:T(8,128)} %bitcast.14, f32[512,128]{1,0:T(8,128)} %bitcast.15, f32[512,128]{1,0:T(8,128)} %bitcast.16, f32[512,128]{1,0:T(8,128)} %bitcast.17, f32[512,128]{1,0:T(8,128)} %bitcast.18, f32[512,128]{1,0:T(8,128)} %bitcast.19, f32[512,128]{1,0:T(8,128)} %bitcast.20, ...), custom_call_target="tpu_custom_call" | custom-call | tf_op jit(solution)/shard_map/pallas_call | solution.py:711
  139.7 0.0 copy-start
  139.8 0.6 copy-done
  140.3 0.5 slice_bitcast_fusion
  140.8 1.7 %copy.15 = f32[1,512,128]{2,1,0:T(8,128)} copy(f32[1,512,128]{2,1,0:T(8,128)} %bitcast.13) | data formatting | bytes 524288
Async XLA Ops:
  139.7 0.6 copy-start

commit v4 on v3

--- a/solution.py
+++ b/solution.py
@@ -14,8 +14,10 @@
 (
     T_TY, T_ST, T_SEED, T_B0, T_RW, T_B1, T_LATE1, T_P1, T_W, T_TIN,
     T_PNEXT, T_FLUX, T_CELL_P, T_CELL_N, T_SLOT, T_VAL, T_MSG_P, T_MSG_N,
-    T_COEF, T_S0, T_S1, T_S2, T_S3, T_R0, T_R1, T_R2, T_R3, T_PART, T_COUNT,
-) = range(29)
+    T_COEF, T_S0, T_S1, T_S2, T_S3, T_R0, T_R1, T_R2, T_R3, T_PART, T_PIECE, T_COUNT_BASE,
+) = range(30)
+PIECES = 4
+T_COUNT = T_PIECE + 2 * PIECES
 L_SRC, L_P0, L_TX, L_TY, L_TZ, L_ST, L_COUNT = range(7)
 
 
@@ -172,7 +174,13 @@
 
     to_y(T_TY, trans_y, ty_y)
     to_y(T_ST, storage, st_y)
-    remote(pressure, p_next, T_PNEXT, prev_dev).start()
+    piece = nx // PIECES
+
+    def part(ref, i):
+        return ref.at[pl.ds(i * piece, piece)]
+
+    for i in range(PIECES):
+        remote(part(pressure, i), part(p_next, i), T_PIECE + i, prev_dev).start()
     to_y(T_SEED, seed, seed_y)
     remote(cell_s, cell_r.at[1], T_CELL_P, prev_dev).start()
     remote(cell_s, cell_r.at[0], T_CELL_N, next_dev).start()
@@ -486,42 +494,40 @@
     factor_y()
     spread_wide(T_COEF, coef_s, coef_r)
 
-    arrived(T_PNEXT, p_next)
-
-    def make_flux(o):
-        tz[pl.ds(o, bl), :] = jnp.where(lane < nk - 1, at(tz, o), 0.0)
-        t = jnp.where(open_y, at(ty, o), 0.0)
-        ty[pl.ds(o, bl), :] = t
-        flux[pl.ds(o, bl), :] = t * (at(p0, o) - at(p_next, o))
-
-    each_block(make_flux)
-    remote(flux, f_prev, T_FLUX, next_dev).start()
+    for i in range(PIECES):
+        rows_at = pl.ds(i * piece, piece)
+        arrived(T_PIECE + i, part(p_next, i))
+        tz[rows_at, :] = jnp.where(lane[0:piece] < nk - 1, tz[rows_at, :], 0.0)
+        t = jnp.where(open_y, ty[rows_at, :], 0.0)
+        ty[rows_at, :] = t
+        flux[rows_at, :] = t * (p0[rows_at, :] - p_next[rows_at, :])
+        remote(part(flux, i), part(f_prev, i), T_PIECE + PIECES + i, next_dev).start()
 
     start_y(seed_y, T_SEED, 0, late1_y)
 
+    for i in range(PIECES):
+        arrived(T_PIECE + PIECES + i, part(f_prev, i))
+
+    def rhs_u0(o):
+        ba[pl.ds(o + pad_x, bl), :] = at(src, o) - (at(flux, o) - at(f_prev, o)) - div_z(at(p0, o), o)
+
+    each_block(rhs_u0)
+    solve_x(u0)
+
+    def make_b0(o):
+        b0[pl.ds(o, bl), :] = at(src, o) - div_x(u0, o) - div_z(up(u0, o), o)
+
+    each_block(make_b0)
+    to_y(T_B0, b0, b0_y)
+
+    arrived(T_COEF, coef_r)
+    factor_sep()
+    middle_y(0)
+
+    start_y(b0_y, T_B0, 1, p1_y)
     arrived(T_CELL_P, cell_r.at[1])
     arrived(T_CELL_N, cell_r.at[0])
     prepare_picks()
-
-    arrived(T_FLUX, f_prev)
-
-    def rhs_u0(o):
-        ba[pl.ds(o + pad_x, bl), :] = at(src, o) - (at(flux, o) - at(f_prev, o)) - div_z(at(p0, o), o)
-
-    each_block(rhs_u0)
-    solve_x(u0)
-
-    def make_b0(o):
-        b0[pl.ds(o, bl), :] = at(src, o) - div_x(u0, o) - div_z(up(u0, o), o)
-
-    each_block(make_b0)
-    to_y(T_B0, b0, b0_y)
-
-    arrived(T_COEF, coef_r)
-    factor_sep()
-    middle_y(0)
-
-    start_y(b0_y, T_B0, 1, p1_y)
     end_y(0, late1_y, T_LATE1, late1)
     middle_y(1)
 
@@ -638,8 +644,9 @@
 
     for number in (T_TY, T_ST, T_SEED, T_B0, T_RW, T_B1, T_LATE1, T_P1, T_W):
         sent(number, ty_y.at[pl.ds(0, nn - 1)])
-    sent(T_PNEXT, p_next)
-    sent(T_FLUX, flux)
+    for i in range(PIECES):
+        sent(T_PIECE + i, part(p_next, i))
+        sent(T_PIECE + PIECES + i, part(flux, i))
     sent(T_CELL_P, cell_s)
     sent(T_CELL_N, cell_s)
     sent(T_MSG_P, msg_p)

time: 143 us -> 142 us (level)
  no operation moved by 1% of the time
where the time goes in v4:
time: 142 us; the launch traced here: 141 us
  Pallas kernels  137 us (96%)
  local copies, waits for them, and re-layouts  2.74 us (2%)
    pallas_call x1, Pallas kernels, local(): pl.pallas_call(functools.partial(kernel, nw, nn, nx, nk, cap, owned), out...  137 us

profile of v4, /device:TPU:1, one launch (start us, length us, event | category | flops | bytes accessed | tf_op | source)
XLA Modules:
  0.0 141.5 jit_solution(13462766696111926062)
XLA Ops:
  1.3 137.5 %shard_map.122 = (f32[512,128]{1,0:T(8,128)}, f32[1,128]{1,0:T(1,128)}) custom-call(f32[512,128]{1,0:T(8,128)} %bitcast.14, f32[512,128]{1,0:T(8,128)} %bitcast.15, f32[512,128]{1,0:T(8,128)} %bitcast.16, f32[512,128]{1,0:T(8,128)} %bitcast.17, f32[512,128]{1,0:T(8,128)} %bitcast.18, f32[512,128]{1,0:T(8,128)} %bitcast.19, f32[512,128]{1,0:T(8,128)} %bitcast.20, ...), custom_call_target="tpu_custom_call" | custom-call | tf_op jit(solution)/shard_map/pallas_call | solution.py:718
  138.7 0.0 copy-start
  138.8 0.6 copy-done
  139.3 0.5 slice_bitcast_fusion
  139.8 1.7 %copy.15 = f32[1,512,128]{2,1,0:T(8,128)} copy(f32[1,512,128]{2,1,0:T(8,128)} %bitcast.13) | data formatting | bytes 524288
Async XLA Ops:
  138.7 0.6 copy-start

commit v5 on v4

--- a/solution.py
+++ b/solution.py
@@ -552,8 +552,6 @@
     spread_wide(T_TIN, tin_s, tin_r)
 
     start_y(rw_y, T_RW, 2, w_y)
-    prepare_group()
-    prepare_owners()
 
     arrived(T_P1, inner(p1))
 
@@ -574,6 +572,8 @@
     pick_three(0)
     start_y(b1_y, T_B1, 3, p2_y)
     end_y(2, w_y, T_W, w_x)
+    prepare_group()
+    prepare_owners()
 
     arrived(T_W, inner(w_x))
 

time: 142 us -> 142 us (level)
  no operation moved by 1% of the time
where the time goes in v5:
time: 142 us; the launch traced here: 141 us
  Pallas kernels  137 us (96%)
  local copies, waits for them, and re-layouts  2.74 us (2%)
    pallas_call x1, Pallas kernels, local(): pl.pallas_call(functools.partial(kernel, nw, nn, nx, nk, cap, owned), out...  137 us

profile of v5, /device:TPU:1, one launch (start us, length us, event | category | flops | bytes accessed | tf_op | source)
XLA Modules:
  0.0 141.5 jit_solution(15725063738756937850)
XLA Ops:
  1.3 137.4 %shard_map.122 = (f32[512,128]{1,0:T(8,128)}, f32[1,128]{1,0:T(1,128)}) custom-call(f32[512,128]{1,0:T(8,128)} %bitcast.14, f32[512,128]{1,0:T(8,128)} %bitcast.15, f32[512,128]{1,0:T(8,128)} %bitcast.16, f32[512,128]{1,0:T(8,128)} %bitcast.17, f32[512,128]{1,0:T(8,128)} %bitcast.18, f32[512,128]{1,0:T(8,128)} %bitcast.19, f32[512,128]{1,0:T(8,128)} %bitcast.20, ...), custom_call_target="tpu_custom_call" | custom-call | tf_op jit(solution)/shard_map/pallas_call | solution.py:718
  138.7 0.0 copy-start
  138.7 0.6 copy-done
  139.3 0.5 slice_bitcast_fusion
  139.8 1.7 %copy.15 = f32[1,512,128]{2,1,0:T(8,128)} copy(f32[1,512,128]{2,1,0:T(8,128)} %bitcast.13) | data formatting | bytes 524288
Async XLA Ops:
  138.7 0.6 copy-start
